TPU v7x, 512 devices: a whole 4x8x8 slice. The times are simulated.
512 devices in a mesh: seq: 16 (over y, core), grp: 32 (over z, x).
Axes of the slice: x: 4, y: 8, z: 8, core: 2. Of those that a mesh axis runs over, the one named last changes fastest.
Arguments:
- queries: bfloat16 [65536, 1024], P(('seq', 'grp')), as said below
- key_rows: bfloat16 [65536, 1024], P(('seq', 'grp')), as said below
- value_rows: bfloat16 [65536, 1024], P(('seq', 'grp')), may hold values from -6 to 6
- cotangent: bfloat16 [65536, 1024], P(('seq', 'grp')), may hold values from -6 to 6
- out_weight: bfloat16 [1024, 1024], replicated, may hold values from -0.1875 to 0.1875
- send_lists: int32 [32, 32, 1], P('grp'), may hold values from 0 to 15
- key_blocks: int32 [32, 16, 8], P('grp'), may hold values from 0 to 47, as said below
- key_counts: int32 [32, 16], P('grp'), may hold values from 1 to 8, as said below
Outputs:
- layer_out: bfloat16 [65536, 1024], P(('seq', 'grp'))
- query_grad: bfloat16 [65536, 1024], P(('seq', 'grp'))
- key_grad: bfloat16 [65536, 1024], P(('seq', 'grp'))
- value_grad: bfloat16 [65536, 1024], P(('seq', 'grp'))
- weight_grad: float32 [1024, 1024], P('grp')
Inputs may be any that keep to these rules, and one draw needn't show every extreme that they name: `queries`: entries within -6 to 6. `key_rows`: entries within -6 to 6. `key_blocks`: the first listed block of query block b of a group is block b of that group itself; entries at t >= the block's count are unused. `key_counts`: every group has a query block with all 8 listed blocks live.
All inputs are finite; a program needn't handle non-finite values.
Results may differ from a plain program's by a relative error of at most 0.015.
Values may be sent and summed in bfloat16 or wider, within the bound.
A program may use at most 64 MiB of HBM per device.

v0:
```python
import math

import jax
import jax.numpy as jnp
from jax import lax
from jax.sharding import PartitionSpec as P

HEADS = 16


def span_step(query_blk, extended, list_rows, counts, grad_blk, score_scale):
    chosen = extended[list_rows]
    listed_shape = chosen.shape
    key_width = listed_shape[1] * listed_shape[2]
    chosen = chosen.reshape(listed_shape[0], key_width, 2, listed_shape[4], listed_shape[5])
    key_part = chosen[:, :, 0]
    value_part = chosen[:, :, 1]
    scores = (
        jnp.einsum("cihe,cjhe->chij", query_blk, key_part, preferred_element_type=jnp.float32)
        * score_scale
    )
    column = jnp.arange(key_width, dtype=jnp.int32) // listed_shape[2]
    live_mask = column[None, :] < counts[:, None]
    scores = jnp.where(live_mask[:, None, None, :], scores, -jnp.inf)
    row_top = jnp.max(scores, axis=-1, keepdims=True)
    weights = jnp.exp(scores - row_top)
    prob_full = weights / jnp.sum(weights, axis=-1, keepdims=True)
    probs_low = prob_full.astype(jnp.bfloat16)
    attended = jnp.einsum(
        "chij,cjhe->cihe", probs_low, value_part, preferred_element_type=jnp.float32
    ).astype(jnp.bfloat16)
    dprobs = jnp.einsum("cihe,cjhe->chij", grad_blk, value_part, preferred_element_type=jnp.float32)
    row_inner = jnp.sum(prob_full * dprobs, axis=-1, keepdims=True)
    dscores = (prob_full * (dprobs - row_inner) * score_scale).astype(jnp.bfloat16)
    dquery = jnp.einsum(
        "chij,cjhe->cihe", dscores, key_part, preferred_element_type=jnp.float32
    ).astype(jnp.bfloat16)
    key_grad = jnp.einsum("chij,cihe->cjhe", dscores, query_blk, preferred_element_type=jnp.float32)
    dvalue = jnp.einsum("chij,cihe->cjhe", probs_low, grad_blk, preferred_element_type=jnp.float32)
    pair_grad = jnp.stack((key_grad, dvalue), axis=2).reshape(listed_shape)
    return (attended, dquery, pair_grad)


def group_pass(query_rows, extended, list_rows, counts, grad_rows):
    group_blocks = list_rows.shape[0]
    block_rows = extended.shape[1]
    head_count = query_rows.shape[1]
    head_size = query_rows.shape[2]
    group_size = math.gcd(group_blocks, max(1, 512 // block_rows))
    steps_count = group_blocks // group_size
    score_scale = 1.0 / math.sqrt(head_size)
    query_steps = query_rows.reshape(steps_count, group_size, block_rows, head_count, head_size)
    grad_steps = grad_rows.reshape(steps_count, group_size, block_rows, head_count, head_size)
    list_steps = list_rows.reshape(steps_count, group_size, list_rows.shape[1])
    count_steps = counts.reshape(steps_count, group_size)

    def advance(grad_total, pieces):
        query_blk, list_blk, count_blk, grad_blk = pieces
        attended, dquery, pair_grad = span_step(
            query_blk, extended, list_blk, count_blk, grad_blk, score_scale
        )
        grad_total = grad_total.at[list_blk].add(pair_grad)
        return (grad_total, (attended, dquery))

    start_total = jnp.zeros(extended.shape, jnp.float32)
    grad_total, outputs = lax.scan(
        advance, start_total, (query_steps, list_steps, count_steps, grad_steps)
    )
    attended = outputs[0].reshape(group_blocks * block_rows, head_count * head_size)
    dquery = outputs[1].reshape(group_blocks * block_rows, head_count * head_size)
    return (attended, dquery, grad_total)


def per_device(
    queries, key_rows, value_rows, cotangent, out_weight, send_lists, key_blocks, key_counts
):
    seq_count = lax.axis_size("seq")
    grp_count = lax.axis_size("grp")
    rows_dev = queries.shape[0]
    model_width = queries.shape[1]
    head_size = model_width // HEADS
    incoming_grad = jnp.einsum(
        "nf,df->nd", cotangent, out_weight, preferred_element_type=jnp.float32
    ).astype(jnp.bfloat16)
    head_query, head_key, head_value, head_grad = (
        lax.all_to_all(queries, "seq", split_axis=1, concat_axis=0, tiled=True),
        lax.all_to_all(key_rows, "seq", split_axis=1, concat_axis=0, tiled=True),
        lax.all_to_all(value_rows, "seq", split_axis=1, concat_axis=0, tiled=True),
        lax.all_to_all(incoming_grad, "seq", split_axis=1, concat_axis=0, tiled=True),
    )
    list_local = key_blocks[0]
    count_local = key_counts[0]
    send_local = send_lists[0]
    group_blocks = list_local.shape[0]
    group_rows = head_query.shape[0]
    block_rows = group_rows // group_blocks
    heads_dev = head_query.shape[1] // head_size
    stacked = jnp.concatenate((head_key, head_value), axis=1)
    pair_width = stacked.shape[1]
    own_blocks = stacked.reshape(group_blocks, block_rows, pair_width)
    outgoing = own_blocks[send_local]
    incoming = lax.all_to_all(outgoing, "grp", split_axis=0, concat_axis=0, tiled=True)
    extended = jnp.concatenate((own_blocks, incoming.reshape(-1, block_rows, pair_width)), axis=0)
    extended = extended.reshape(extended.shape[0], block_rows, 2, heads_dev, head_size)
    attended, dquery, grad_total = group_pass(
        head_query.reshape(group_rows, heads_dev, head_size),
        extended,
        list_local,
        count_local,
        head_grad.reshape(group_rows, heads_dev, head_size),
    )
    grad_total = grad_total.reshape(grad_total.shape[0], block_rows, pair_width)
    own_grad = grad_total[:group_blocks]
    halo_grad = grad_total[group_blocks:].reshape(grp_count, -1, block_rows, pair_width)
    returned = lax.all_to_all(
        halo_grad.astype(jnp.bfloat16), "grp", split_axis=0, concat_axis=0, tiled=True
    ).astype(halo_grad.dtype)
    own_grad = own_grad.at[send_local].add(returned)
    grad_low = own_grad.astype(jnp.bfloat16).reshape(group_rows, pair_width)
    half_width = pair_width // 2
    key_part = grad_low[:, :half_width]
    value_part = grad_low[:, half_width:]
    node_attended, query_grad, key_grad, value_grad = (
        lax.all_to_all(attended, "seq", split_axis=0, concat_axis=1, tiled=True),
        lax.all_to_all(dquery, "seq", split_axis=0, concat_axis=1, tiled=True),
        lax.all_to_all(key_part, "seq", split_axis=0, concat_axis=1, tiled=True),
        lax.all_to_all(value_part, "seq", split_axis=0, concat_axis=1, tiled=True),
    )
    layer_out = jnp.dot(node_attended, out_weight, preferred_element_type=jnp.float32).astype(
        jnp.bfloat16
    )
    inverse_root = 1.0 / math.sqrt(float(rows_dev * seq_count * grp_count))
    share_rows = model_width // grp_count
    local_term = (
        jnp.einsum("nd,ne->de", node_attended, cotangent, preferred_element_type=jnp.float32)
        * inverse_root
    )
    summed = lax.psum(local_term, ("seq", "grp"))
    weight_grad = lax.dynamic_slice_in_dim(
        summed, lax.axis_index("grp") * share_rows, share_rows, 0
    )
    return (layer_out, query_grad, key_grad, value_grad, weight_grad)


def solution(mesh):
    in_specs = (
        P(("seq", "grp"), None),
        P(("seq", "grp"), None),
        P(("seq", "grp"), None),
        P(("seq", "grp"), None),
        P(),
        P("grp", None, None),
        P("grp", None, None),
        P("grp", None),
    )
    out_specs = (
        P(("seq", "grp"), None),
        P(("seq", "grp"), None),
        P(("seq", "grp"), None),
        P(("seq", "grp"), None),
        P("grp", None),
    )
    return jax.shard_map(
        per_device, mesh=mesh, in_specs=in_specs, out_specs=out_specs, check_vma=False
    )
```

profile of v0, /device:TPU:1, one launch (start us, length us, event | category | flops | bytes accessed | tf_op | source)
XLA Modules:
  0.0 612.6 jit_solution(3851991760636936697)
XLA Ops:
  9.1 10.2 %all-to-all-start.1 = ((bf16[128,16,64]{0,2,1:T(8,128)(2,1)}), bf16[128,16,64]{0,2,1:T(8,128)(2,1)S(1)}, u32[]{:S(2)}, u32[]{:S(2)}) async-start(bf16[128,16,64]{0,2,1:T(8,128)(2,1)} %bitcast.25), calls=%async_computation.1 | async-start | bytes 524288 | tf_op jit(solution)/shard_map/all_to_all | solution.py:87
  21.1 10.1 %all-to-all-done.1 = bf16[128,16,64]{0,2,1:T(8,128)(2,1)S(1)} async-done(((bf16[128,16,64]{0,2,1:T(8,128)(2,1)}), bf16[128,16,64]{0,2,1:T(8,128)(2,1)S(1)}, u32[]{:S(2)}, u32[]{:S(2)}) %all-to-all-start.1) | async-done | bytes 262176 | tf_op jit(solution)/shard_map/all_to_all | solution.py:87
  31.2 3.4 all-to-all-start.2
  35.5 10.2 %all-to-all-done.2 = bf16[128,16,64]{0,2,1:T(8,128)(2,1)S(1)} async-done(((bf16[128,16,64]{0,2,1:T(8,128)(2,1)}), bf16[128,16,64]{0,2,1:T(8,128)(2,1)S(1)}, u32[]{:S(2)}, u32[]{:S(2)}) %all-to-all-start.2) | async-done | bytes 262176 | tf_op jit(solution)/shard_map/all_to_all | solution.py:88
  45.7 3.4 all-to-all-start
  50.8 9.7 %all-to-all-done = bf16[128,16,64]{0,2,1:T(8,128)(2,1)S(1)} async-done(((bf16[128,16,64]{0,2,1:T(8,128)(2,1)}), bf16[128,16,64]{0,2,1:T(8,128)(2,1)S(1)}, u32[]{:S(2)}, u32[]{:S(2)}) %all-to-all-start) | async-done | bytes 262176 | tf_op jit(solution)/shard_map/all_to_all | solution.py:86
  61.2 11.5 %all-to-all-start.3 = ((bf16[32,1,128,128]{2,3,1,0:T(8,128)(2,1)}), bf16[32,1,128,128]{2,3,1,0:T(8,128)(2,1)S(1)}, u32[]{:S(2)}, u32[]{:S(2)}) async-start(bf16[32,1,128,128]{2,3,1,0:T(8,128)(2,1)} %bitcast.194), calls=%async_computation.3 | async-start | bytes 2097152 | tf_op jit(solution)/shard_map/all_to_all | solution.py:102
  77.1 23.0 %all-to-all-done.3 = bf16[32,1,128,128]{2,3,1,0:T(8,128)(2,1)S(1)} async-done(((bf16[32,1,128,128]{2,3,1,0:T(8,128)(2,1)}), bf16[32,1,128,128]{2,3,1,0:T(8,128)(2,1)S(1)}, u32[]{:S(2)}, u32[]{:S(2)}) %all-to-all-start.3) | async-done | bytes 1048608 | tf_op jit(solution)/shard_map/all_to_all | solution.py:102
  100.1 5.5 all-to-all-start.4
  109.2 8.4 %all-to-all-done.4 = bf16[128,16,64]{0,2,1:T(8,128)(2,1)} async-done(((bf16[128,16,64]{0,2,1:T(8,128)(2,1)}), bf16[128,16,64]{0,2,1:T(8,128)(2,1)}, u32[]{:S(2)}, u32[]{:S(2)}) %all-to-all-start.4) | async-done | bytes 262176 | tf_op jit(solution)/shard_map/all_to_all | solution.py:89
  119.7 168.4 %while.16 = (s32[]{:T(128)}, f32[48,128,2,1,64]{1,4,2,0,3:T(8,128)}, bf16[4,4,128,1,64]{2,4,1,3,0:T(8,128)(2,1)}, bf16[4,4,128,1,64]{2,4,1,3,0:T(8,128)(2,1)}, s...) while((s32[]{:T(128)}, ...), condition=%wide.region_5.6_spmd, body=%wide.region_0.5_spmd.sunk | while | flops 415319136 | bytes 69635216 | solution.py:66
  126.4 3.3 fusion.102
  129.7 2.9 fusion.106
  134.9 2.6 fusion.104
  137.5 6.8 %fusion.107 = bf16[4,4,128,1,64]{2,4,1,3,0:T(8,128)(2,1)} fusion(bf16[4,4,128,1,64]{2,4,1,3,0:T(8,128)(2,1)} %get-tuple-element.280, s32[]{:T(128)S(6)} %copy.160, f32[4,128,1024]{2,1,0:T(8,128)} %fusion.104, bf16[4,1024,1,1,64]{1,0,4,2,3:T(4,128)(2,1)} %get-tuple-element.263, f32[4,128,1024]{2,1,0:T(8,128)} %get-tuple-element.264, ...), kind=kOutput, calls=%fused_computation.20.clone.1 | convolution fusion | flops 70813184 | bytes 8982532 | tf_op jit(solution)/shard_map/while/body/eval_jaxpr/chij,cjhe->cihe/dot_general | solution.py:35
  144.3 7.1 %fusion.105 = f32[4,64,1024]{2,1,0:T(8,128)} fusion(f32[4,128,1024]{2,1,0:T(8,128)} %fusion.104, bf16[4,4,128,1,64]{2,4,1,3,0:T(8,128)(2,1)S(1)} %get-tuple-element.292, s32[]{:T(128)S(6)} %copy.160, f32[4,128,1024]{2,1,0:T(8,128)} %get-tuple-element.264, f32[4,128]{1,0:T(4,128)S(1)} %get-tuple-element.265), kind=kOutput, calls=%fused_computation.14.clone.1 | convolution fusion | flops 70780416 | bytes 9506820 | tf_op jit(solution)/shard_map/while/body/eval_jaxpr/chij,cihe->cjhe/dot_general | solution.py:38
  154.7 7.0 %scatter_fusion = f32[48,128,2,64]{1,3,2,0:T(8,128)} fusion(f32[48,128,2,64]{1,3,2,0:T(8,128)} %bitcast.185, s32[32]{0:T(128)S(1)} %reshape.368, f32[32,128,2,64]{1,3,2,0:T(8,128)} %bitcast.184), kind=kCustom, calls=%fused_computation.2.clone.1 | custom fusion | flops 524288 | bytes 6291584 | tf_op jit(solution)/shard_map/while/body/eval_jaxpr/scatter-add | solution.py:62
  168.4 3.3 fusion.102
  171.7 2.9 fusion.106
  176.9 2.6 fusion.104
  179.6 6.8 %fusion.107 = bf16[4,4,128,1,64]{2,4,1,3,0:T(8,128)(2,1)} fusion(bf16[4,4,128,1,64]{2,4,1,3,0:T(8,128)(2,1)} %get-tuple-element.280, s32[]{:T(128)S(6)} %copy.160, f32[4,128,1024]{2,1,0:T(8,128)} %fusion.104, bf16[4,1024,1,1,64]{1,0,4,2,3:T(4,128)(2,1)} %get-tuple-element.263, f32[4,128,1024]{2,1,0:T(8,128)} %get-tuple-element.264, ...), kind=kOutput, calls=%fused_computation.20.clone.1 | convolution fusion | flops 70813184 | bytes 8982532 | tf_op jit(solution)/shard_map/while/body/eval_jaxpr/chij,cjhe->cihe/dot_general | solution.py:35
  186.3 7.1 %fusion.105 = f32[4,64,1024]{2,1,0:T(8,128)} fusion(f32[4,128,1024]{2,1,0:T(8,128)} %fusion.104, bf16[4,4,128,1,64]{2,4,1,3,0:T(8,128)(2,1)S(1)} %get-tuple-element.292, s32[]{:T(128)S(6)} %copy.160, f32[4,128,1024]{2,1,0:T(8,128)} %get-tuple-element.264, f32[4,128]{1,0:T(4,128)S(1)} %get-tuple-element.265), kind=kOutput, calls=%fused_computation.14.clone.1 | convolution fusion | flops 70780416 | bytes 9506820 | tf_op jit(solution)/shard_map/while/body/eval_jaxpr/chij,cihe->cjhe/dot_general | solution.py:38
  196.8 7.1 %scatter_fusion = f32[48,128,2,64]{1,3,2,0:T(8,128)} fusion(f32[48,128,2,64]{1,3,2,0:T(8,128)} %bitcast.185, s32[32]{0:T(128)S(1)} %reshape.368, f32[32,128,2,64]{1,3,2,0:T(8,128)} %bitcast.184), kind=kCustom, calls=%fused_computation.2.clone.1 | custom fusion | flops 524288 | bytes 6291584 | tf_op jit(solution)/shard_map/while/body/eval_jaxpr/scatter-add | solution.py:62
  210.6 3.3 fusion.102
  213.9 2.9 fusion.106
  221.7 6.8 %fusion.107 = bf16[4,4,128,1,64]{2,4,1,3,0:T(8,128)(2,1)} fusion(bf16[4,4,128,1,64]{2,4,1,3,0:T(8,128)(2,1)} %get-tuple-element.280, s32[]{:T(128)S(6)} %copy.160, f32[4,128,1024]{2,1,0:T(8,128)} %fusion.104, bf16[4,1024,1,1,64]{1,0,4,2,3:T(4,128)(2,1)} %get-tuple-element.263, f32[4,128,1024]{2,1,0:T(8,128)} %get-tuple-element.264, ...), kind=kOutput, calls=%fused_computation.20.clone.1 | convolution fusion | flops 70813184 | bytes 8982532 | tf_op jit(solution)/shard_map/while/body/eval_jaxpr/chij,cjhe->cihe/dot_general | solution.py:35
  228.5 7.1 %fusion.105 = f32[4,64,1024]{2,1,0:T(8,128)} fusion(f32[4,128,1024]{2,1,0:T(8,128)} %fusion.104, bf16[4,4,128,1,64]{2,4,1,3,0:T(8,128)(2,1)S(1)} %get-tuple-element.292, s32[]{:T(128)S(6)} %copy.160, f32[4,128,1024]{2,1,0:T(8,128)} %get-tuple-element.264, f32[4,128]{1,0:T(4,128)S(1)} %get-tuple-element.265), kind=kOutput, calls=%fused_computation.14.clone.1 | convolution fusion | flops 70780416 | bytes 9506820 | tf_op jit(solution)/shard_map/while/body/eval_jaxpr/chij,cihe->cjhe/dot_general | solution.py:38
  238.9 7.1 %scatter_fusion = f32[48,128,2,64]{1,3,2,0:T(8,128)} fusion(f32[48,128,2,64]{1,3,2,0:T(8,128)} %bitcast.185, s32[32]{0:T(128)S(1)} %reshape.368, f32[32,128,2,64]{1,3,2,0:T(8,128)} %bitcast.184), kind=kCustom, calls=%fused_computation.2.clone.1 | custom fusion | flops 524288 | bytes 6291584 | tf_op jit(solution)/shard_map/while/body/eval_jaxpr/scatter-add | solution.py:62
  252.6 3.3 fusion.102
  255.9 2.9 fusion.106
  261.1 2.6 fusion.104
  263.8 6.8 %fusion.107 = bf16[4,4,128,1,64]{2,4,1,3,0:T(8,128)(2,1)} fusion(bf16[4,4,128,1,64]{2,4,1,3,0:T(8,128)(2,1)} %get-tuple-element.280, s32[]{:T(128)S(6)} %copy.160, f32[4,128,1024]{2,1,0:T(8,128)} %fusion.104, bf16[4,1024,1,1,64]{1,0,4,2,3:T(4,128)(2,1)} %get-tuple-element.263, f32[4,128,1024]{2,1,0:T(8,128)} %get-tuple-element.264, ...), kind=kOutput, calls=%fused_computation.20.clone.1 | convolution fusion | flops 70813184 | bytes 8982532 | tf_op jit(solution)/shard_map/while/body/eval_jaxpr/chij,cjhe->cihe/dot_general | solution.py:35
  270.5 7.1 %fusion.105 = f32[4,64,1024]{2,1,0:T(8,128)} fusion(f32[4,128,1024]{2,1,0:T(8,128)} %fusion.104, bf16[4,4,128,1,64]{2,4,1,3,0:T(8,128)(2,1)S(1)} %get-tuple-element.292, s32[]{:T(128)S(6)} %copy.160, f32[4,128,1024]{2,1,0:T(8,128)} %get-tuple-element.264, f32[4,128]{1,0:T(4,128)S(1)} %get-tuple-element.265), kind=kOutput, calls=%fused_computation.14.clone.1 | convolution fusion | flops 70780416 | bytes 9506820 | tf_op jit(solution)/shard_map/while/body/eval_jaxpr/chij,cihe->cjhe/dot_general | solution.py:38
  281.0 7.1 %scatter_fusion = f32[48,128,2,64]{1,3,2,0:T(8,128)} fusion(f32[48,128,2,64]{1,3,2,0:T(8,128)} %bitcast.185, s32[32]{0:T(128)S(1)} %reshape.368, f32[32,128,2,64]{1,3,2,0:T(8,128)} %bitcast.184), kind=kCustom, calls=%fused_computation.2.clone.1 | custom fusion | flops 524288 | bytes 6291584 | tf_op jit(solution)/shard_map/while/body/eval_jaxpr/scatter-add | solution.py:62
  288.0 3.4 all-to-all-start.5
  294.6 7.9 %all-to-all-done.5 = bf16[16,128,64]{1,2,0:T(8,128)(2,1)S(1)} async-done(((bf16[16,128,64]{1,2,0:T(8,128)(2,1)}), bf16[16,128,64]{1,2,0:T(8,128)(2,1)S(1)}, u32[]{:S(2)}, u32[]{:S(2)}) %all-to-all-start.5) | async-done | bytes 262176 | tf_op jit(solution)/shard_map/all_to_all | solution.py:124
  302.5 5.2 all-to-all-start.7
  307.8 2.7 convolution_multiply_fusion
  314.4 22.2 %all-to-all-done.7 = bf16[32,1,128,128]{3,2,1,0:T(8,128)(2,1)} async-done(((bf16[32,1,128,128]{3,2,1,0:T(8,128)(2,1)}), bf16[32,1,128,128]{3,2,1,0:T(8,128)(2,1)}, u32[]{:S(2)}, u32[]{:S(2)}) %all-to-all-start.7) | async-done | bytes 1048608 | tf_op jit(solution)/shard_map/all_to_all | solution.py:115
  336.5 5.4 all-to-all-start.6
  342.0 2.9 bitcast_convert_fusion
  344.8 4.7 scatter_fusion.1
  350.7 3.1 all-to-all-done.6
  353.8 4.2 all-to-all-start.8
  358.9 11.9 %all-to-all-done.8 = bf16[16,128,64]{1,2,0:T(8,128)(2,1)S(1)} async-done(((bf16[16,128,64]{1,2,0:T(8,128)(2,1)}), bf16[16,128,64]{1,2,0:T(8,128)(2,1)S(1)}, u32[]{:S(2)}, u32[]{:S(2)}) %all-to-all-start.8) | async-done | bytes 262176 | tf_op jit(solution)/shard_map/all_to_all | solution.py:126
  370.7 3.4 all-to-all-start.9
  378.0 7.0 %all-to-all-done.9 = bf16[16,128,64]{1,2,0:T(8,128)(2,1)S(1)} async-done(((bf16[16,128,64]{1,2,0:T(8,128)(2,1)}), bf16[16,128,64]{1,2,0:T(8,128)(2,1)S(1)}, u32[]{:S(2)}, u32[]{:S(2)}) %all-to-all-start.9) | async-done | bytes 262176 | tf_op jit(solution)/shard_map/all_to_all | solution.py:127
  385.9 218.4 %all-reduce.2.cloned.1.call-done = f32[1024,1024]{1,0:T(8,128)} async-done(((f32[1024,1024]{1,0:T(8,128)}), f32[1024,1024]{1,0:T(8,128)}) %all-reduce.2.cloned.1.call-update) | async-done | bytes 4194320 | tf_op jit(solution)/shard_map/psum | solution.py:138
  (135 shorter events, 84.1 us)
Async XLA Ops:
  7.2 65.6 %copy-start = (bf16[1024,1024]{1,0:T(8,128)(2,1)S(1)}, bf16[1024,1024]{1,0:T(8,128)(2,1)}, u32[]{:S(2)}) copy-start(bf16[1024,1024]{1,0:T(8,128)(2,1)} %param.14) | copy-start | bytes 6291460
  7.2 27.5 %copy-start.5 = (bf16[128,1024]{1,0:T(8,128)(2,1)S(1)}, bf16[128,1024]{1,0:T(8,128)(2,1)}, u32[]{:S(2)}) copy-start(bf16[128,1024]{1,0:T(8,128)(2,1)} %param.10) | copy-start | bytes 786436
  7.2 41.9 %copy-start.9 = (s32[1,32,1]{1,2,0:T(1,128)S(1)}, s32[1,32,1]{1,2,0:T(1,128)}, u32[]{:S(2)}) copy-start(s32[1,32,1]{1,2,0:T(1,128)} %param.15) | copy-start | bytes 388
  9.1 22.1 %all-to-all-start.1 = ((bf16[128,16,64]{0,2,1:T(8,128)(2,1)}), bf16[128,16,64]{0,2,1:T(8,128)(2,1)S(1)}, u32[]{:S(2)}, u32[]{:S(2)}) async-start(bf16[128,16,64]{0,2,1:T(8,128)(2,1)} %bitcast.25), calls=%async_computation.1 | async-start | bytes 524288 | tf_op jit(solution)/shard_map/all_to_all | solution.py:87
  31.2 14.5 %all-to-all-start.2 = ((bf16[128,16,64]{0,2,1:T(8,128)(2,1)}), bf16[128,16,64]{0,2,1:T(8,128)(2,1)S(1)}, u32[]{:S(2)}, u32[]{:S(2)}) async-start(bf16[128,16,64]{0,2,1:T(8,128)(2,1)} %bitcast.28), calls=%async_computation.2 | async-start | bytes 524288 | tf_op jit(solution)/shard_map/all_to_all | solution.py:88
  45.7 14.9 %copy-start.3 = (bf16[128,16,64]{0,2,1:T(8,128)(2,1)}, bf16[128,16,64]{0,2,1:T(8,128)(2,1)S(1)}, u32[]{:S(2)}) copy-start(bf16[128,16,64]{0,2,1:T(8,128)(2,1)S(1)} %all-to-all-done.2) | copy-start | bytes 786436
  45.7 14.9 %all-to-all-start = ((bf16[128,16,64]{0,2,1:T(8,128)(2,1)}), bf16[128,16,64]{0,2,1:T(8,128)(2,1)S(1)}, u32[]{:S(2)}, u32[]{:S(2)}) async-start(bf16[128,16,64]{0,2,1:T(8,128)(2,1)} %bitcast.21), calls=%async_computation | async-start | bytes 524288 | tf_op jit(solution)/shard_map/all_to_all | solution.py:86
  60.5 0.7 copy-start.6
  61.2 38.9 %all-to-all-start.3 = ((bf16[32,1,128,128]{2,3,1,0:T(8,128)(2,1)}), bf16[32,1,128,128]{2,3,1,0:T(8,128)(2,1)S(1)}, u32[]{:S(2)}, u32[]{:S(2)}) async-start(bf16[32,1,128,128]{2,3,1,0:T(8,128)(2,1)} %bitcast.194), calls=%async_computation.3 | async-start | bytes 2097152 | tf_op jit(solution)/shard_map/all_to_all | solution.py:102
  72.8 33.3 %copy-start.10 = (s32[1,16]{1,0:T(1,128)S(1)}, s32[1,16]{1,0:T(1,128)}, u32[]{:S(2)}) copy-start(s32[1,16]{1,0:T(1,128)} %param.17) | copy-start | bytes 196
  72.8 34.0 %copy-start.8 = (s32[1,16,8]{1,2,0:T(8,128)S(1)}, s32[1,16,8]{1,2,0:T(8,128)}, u32[]{:S(2)}) copy-start(s32[1,16,8]{1,2,0:T(8,128)} %param.16) | copy-start | bytes 1540
  100.1 17.5 %all-to-all-start.4 = ((bf16[128,16,64]{0,2,1:T(8,128)(2,1)}), bf16[128,16,64]{0,2,1:T(8,128)(2,1)}, u32[]{:S(2)}, u32[]{:S(2)}) async-start(bf16[128,16,64]{0,2,1:T(8,128)(2,1)} %bitcast.207), calls=%async_computation.4 | async-start | bytes 524288 | tf_op jit(solution)/shard_map/all_to_all | solution.py:89
  109.2 10.5 %copy-start.7 = (bf16[128,16,64]{0,2,1:T(8,128)(2,1)S(1)}, bf16[128,16,64]{0,2,1:T(8,128)(2,1)}, u32[]{:S(2)}) copy-start(bf16[128,16,64]{0,2,1:T(8,128)(2,1)} %copy-done.6) | copy-start | bytes 786436
  126.4 3.3 copy-start.1
  129.7 2.9 copy-start.11
  133.8 1.0 copy-start.2
  168.4 3.3 copy-start.1
  171.7 2.9 copy-start.11
  175.9 1.0 copy-start.2
  210.6 3.3 copy-start.1
  213.9 2.9 copy-start.11
  218.0 1.0 copy-start.2
  252.6 3.3 copy-start.1
  255.9 2.9 copy-start.11
  260.1 1.0 copy-start.2
  288.0 14.5 %all-to-all-start.5 = ((bf16[16,128,64]{1,2,0:T(8,128)(2,1)}), bf16[16,128,64]{1,2,0:T(8,128)(2,1)S(1)}, u32[]{:S(2)}, u32[]{:S(2)}) async-start(bf16[16,128,64]{1,2,0:T(8,128)(2,1)} %bitcast.210), calls=%async_computation.5 | async-start | bytes 524288 | tf_op jit(solution)/shard_map/all_to_all | solution.py:124
  294.6 13.2 %copy-start.4 = (bf16[128,1024]{1,0:T(8,128)(2,1)S(1)}, bf16[128,1024]{1,0:T(8,128)(2,1)}, u32[]{:S(2)}) copy-start(bf16[128,1024]{1,0:T(8,128)(2,1)} %param.13) | copy-start | bytes 786436
  302.5 34.0 %all-to-all-start.7 = ((bf16[32,1,128,128]{3,2,1,0:T(8,128)(2,1)}), bf16[32,1,128,128]{3,2,1,0:T(8,128)(2,1)}, u32[]{:S(2)}, u32[]{:S(2)}) async-start(bf16[32,1,128,128]{3,2,1,0:T(8,128)(2,1)} %copy.104), calls=%async_computation.7 | async-start | bytes 2097152 | tf_op jit(solution)/shard_map/all_to_all | solution.py:115
  307.8 296.5 %all-reduce.2.cloned.1.call-start = ((), (), s32[]{:S(2)}) async-start(), calls=%async_computation.10 | async-start | bytes 8388608 | tf_op jit(solution)/shard_map/psum | solution.py:138
  336.5 17.2 %all-to-all-start.6 = ((bf16[16,128,64]{1,2,0:T(8,128)(2,1)}), bf16[16,128,64]{1,2,0:T(8,128)(2,1)}, u32[]{:S(2)}, u32[]{:S(2)}) async-start(bf16[16,128,64]{1,2,0:T(8,128)(2,1)} %bitcast.209), calls=%async_computation.6 | async-start | bytes 524288 | tf_op jit(solution)/shard_map/all_to_all | solution.py:125
  353.8 16.9 %all-to-all-start.8 = ((bf16[16,128,64]{1,2,0:T(8,128)(2,1)}), bf16[16,128,64]{1,2,0:T(8,128)(2,1)S(1)}, u32[]{:S(2)}, u32[]{:S(2)}) async-start(bf16[16,128,64]{1,2,0:T(8,128)(2,1)} %copy.107), calls=%async_computation.8 | async-start | bytes 524288 | tf_op jit(solution)/shard_map/all_to_all | solution.py:126
  370.7 14.3 %all-to-all-start.9 = ((bf16[16,128,64]{1,2,0:T(8,128)(2,1)}), bf16[16,128,64]{1,2,0:T(8,128)(2,1)S(1)}, u32[]{:S(2)}, u32[]{:S(2)}) async-start(bf16[16,128,64]{1,2,0:T(8,128)(2,1)} %copy.109), calls=%async_computation.9 | async-start | bytes 524288 | tf_op jit(solution)/shard_map/all_to_all | solution.py:127
Sparse Core Ops, SparseCore 0:
  313.6 290.5 all-reduce.1
where the time goes:
time: 616 us; the launch traced here: 613 us
  waiting for transfers between devices  332 us (54%)
  matrix products  102 us (17%)
  local copies, waits for them, and re-layouts  68.6 us (11%)
  starting transfers between devices  55.8 us (9%)
  other arithmetic  40.1 us (7%)
  between operations  14.2 us (2%)
    psum x1, waiting for transfers between devices, per_device(): summed = lax.psum(local_term, ('seq', 'grp'))  218 us
    dot_general x4, matrix products, span_step(): jnp.einsum('chij,cihe->cjhe', dscores, query_blk, preferred_element_type=...  28.3 us
    scatter-add x4, other arithmetic, advance(): grad_total = grad_total.at[list_blk].add(pair_grad)  28.3 us
    dot_general x4, matrix products, span_step(): jnp.einsum('chij,cjhe->cihe', dscores, key_part, preferred_element_type=j...  27 us
    all_to_all x1, waiting for transfers between devices, per_device(): lax.all_to_all(outgoing, 'grp', split_axis=0, concat_axis=0, tiled=True)  23 us
    all_to_all x1, waiting for transfers between devices, per_device(): lax.all_to_all(halo_grad.astype(jnp.bfloat16), 'grp', split_axis=0, conca...  22.2 us
    gather x8, local copies, waits for them, and re-layouts, span_step(): chosen = extended[list_rows]  15.2 us
    sub x4, matrix products, span_step(): weights = jnp.exp(scores - row_top)  13.2 us
  transfers between devices with their start and end apart: 11, of which 11 were waited for; matrix products, arithmetic and copies ran while one was open for 6% of the time, Pallas kernels for 0%

commit v1 on v0

v1 whole, which is shorter than its diff:
```python
import functools
import math

import jax
import jax.numpy as jnp
from jax import lax
from jax.experimental import pallas as pl
from jax.experimental.pallas import tpu as pltpu
from jax.sharding import PartitionSpec as P

HD = 64
LANES = 128
BF = jnp.bfloat16
F32 = jnp.float32
VMEM = pl.BlockSpec(memory_space=pltpu.VMEM)
SMEM = pl.BlockSpec(memory_space=pltpu.SMEM)
LIMIT = 48 * 1024 * 1024


def weave(left, right):
    lane = lax.broadcasted_iota(jnp.int32, left.shape, 1)
    left_f, right_f = left.astype(F32), right.astype(F32)
    first = jnp.where(lane < HD, left_f, pltpu.roll(right_f, HD, 1))
    second = jnp.where(lane < HD, pltpu.roll(left_f, HD, 1), right_f)
    return first, second


def pack_kernel(q_ref, k_ref, v_ref, c_ref, w_ref, kv_ref, qg_ref):
    grad = lax.dot_general(
        c_ref[...], w_ref[...], (((1,), (1,)), ((), ())), preferred_element_type=F32
    ).astype(BF)
    for j in range(kv_ref.shape[0] // 2):
        cols = slice(j * LANES, (j + 1) * LANES)
        first, second = weave(k_ref[:, cols], v_ref[:, cols])
        kv_ref[2 * j] = first.astype(BF)
        kv_ref[2 * j + 1] = second.astype(BF)
        first, second = weave(q_ref[:, cols], grad[:, cols])
        qg_ref[2 * j] = first.astype(BF)
        qg_ref[2 * j + 1] = second.astype(BF)


def attend_kernel(
    list_ref, count_ref, qg_ref, kv_ref, cot_ref, aq_ref, own_ref, halo_ref, term_ref, kv_t, acc, att_t
):
    blocks, rows, _ = qg_ref.shape
    space = kv_ref.shape[0]
    listed = list_ref.shape[1]
    scale = 1.0 / math.sqrt(HD)

    def prepare(i, carry):
        kv_t[i] = kv_ref[i].T
        acc[i] = jnp.zeros(acc.shape[1:], F32)
        return carry

    lax.fori_loop(0, space, prepare, 0, unroll=4)

    def one(b, live):
        qg = qg_ref[b]
        lane = lax.broadcasted_iota(jnp.int32, qg.shape, 1)
        full = qg.astype(F32)
        x = jnp.concatenate(
            (
                jnp.where(lane < HD, full * scale, 0.0).astype(BF),
                jnp.where(lane < HD, 0.0, full).astype(BF),
            ),
            axis=0,
        )
        index = [list_ref[b, t] for t in range(live)]
        keys = jnp.concatenate([kv_ref[i] for i in index], axis=0)
        both = lax.dot_general(keys, x, (((1,), (1,)), ((), ())), preferred_element_type=F32)
        scores, dprobs = both[:, :rows], both[:, rows:]
        weights = jnp.exp(scores - jnp.max(scores, axis=0, keepdims=True))
        inverse = 1.0 / jnp.sum(weights, axis=0, keepdims=True)
        probs = weights * inverse
        inner = jnp.sum(probs * dprobs, axis=0, keepdims=True)
        z = jnp.concatenate((probs * (dprobs - inner), probs), axis=1).astype(BF)
        pair = jnp.dot(z, x, preferred_element_type=F32)
        for t, i in enumerate(index):
            acc[i] += pair[t * rows : (t + 1) * rows]
        turned = jnp.concatenate([kv_t[i] for i in index], axis=1)
        out = jnp.dot(turned, z, preferred_element_type=F32)
        attended = out[HD:, rows:]
        att_t[:, pl.ds(pl.multiple_of(b * rows, rows), rows)] = attended.astype(BF)
        aq_ref[b] = jnp.concatenate((out[:HD, :rows] * scale, attended), axis=0).T.astype(BF)

    def step(b, carry):
        count = count_ref[0, b]
        for live in range(1, listed + 1):
            pl.when(count == live)(functools.partial(one, b, live))
        return carry

    lax.fori_loop(0, blocks, step, 0)
    own_ref[...] = acc[:blocks]
    halo_ref[...] = acc[blocks:].astype(BF)
    term_ref[...] = jnp.dot(att_t[...], cot_ref[...], preferred_element_type=F32)


def settle_kernel(send_ref, own_ref, back_ref, out_ref, acc):
    acc[...] = own_ref[...]

    def add(g, carry):
        i = send_ref[0, g]
        acc[i] += back_ref[g].astype(F32)
        return carry

    lax.fori_loop(0, back_ref.shape[0], add, 0, unroll=4)
    out_ref[...] = acc[...].astype(BF)


def unpack_kernel(aq_ref, kv_ref, w_ref, out_ref, dq_ref, dk_ref, dv_ref, att):
    for j in range(aq_ref.shape[0] // 2):
        cols = slice(j * LANES, (j + 1) * LANES)
        first, second = weave(aq_ref[2 * j], aq_ref[2 * j + 1])
        dq_ref[:, cols] = first.astype(BF)
        att[:, cols] = second.astype(BF)
        first, second = weave(kv_ref[2 * j], kv_ref[2 * j + 1])
        dk_ref[:, cols] = first.astype(BF)
        dv_ref[:, cols] = second.astype(BF)
    out_ref[...] = jnp.dot(att[...], w_ref[...], preferred_element_type=F32).astype(BF)


def shape(dims, kind=BF):
    return jax.ShapeDtypeStruct(dims, kind)


def call(kernel, in_specs, out_shape, scratch=(), **kw):
    return pl.pallas_call(
        kernel,
        in_specs=in_specs,
        out_specs=jax.tree.map(lambda _: VMEM, out_shape),
        out_shape=out_shape,
        scratch_shapes=list(scratch),
        compiler_params=pltpu.CompilerParams(vmem_limit_bytes=LIMIT),
        **kw,
    )


def attend(lists, counts, qg, kv, cot):
    blocks, rows, lanes = qg.shape
    space = kv.shape[0]
    return call(
        attend_kernel,
        [SMEM, SMEM, VMEM, VMEM, VMEM],
        (
            shape((blocks, rows, lanes)),
            shape((blocks, rows, lanes), F32),
            shape((space - blocks, rows, lanes)),
            shape((HD, cot.shape[1]), F32),
        ),
        [
            pltpu.VMEM((space, lanes, rows), BF),
            pltpu.VMEM((space, rows, lanes), F32),
            pltpu.VMEM((HD, blocks * rows), BF),
        ],
    )(lists, counts, qg, kv, cot)


def per_device(
    queries, key_rows, value_rows, cotangent, out_weight, send_lists, key_blocks, key_counts
):
    seq_count = lax.axis_size("seq")
    grp_count = lax.axis_size("grp")
    rows, width = queries.shape
    heads = width // HD
    packed = shape((heads, rows, 2 * HD))
    kv, qg = call(pack_kernel, [VMEM] * 5, (packed, packed))(
        queries, key_rows, value_rows, cotangent, out_weight
    )
    kv = lax.all_to_all(kv, "seq", split_axis=0, concat_axis=0, tiled=True)
    qg = lax.all_to_all(qg, "seq", split_axis=0, concat_axis=0, tiled=True)
    halo = lax.all_to_all(
        kv[send_lists[0, :, 0]], "grp", split_axis=0, concat_axis=0, tiled=True
    )
    cot = lax.all_gather(cotangent, "seq", axis=0, tiled=True)
    aq, own, halo, term = attend(
        key_blocks[0], key_counts, qg, jnp.concatenate((kv, halo), axis=0), cot
    )
    aq = lax.all_to_all(aq, "seq", split_axis=0, concat_axis=0, tiled=True)
    back = lax.all_to_all(halo, "grp", split_axis=0, concat_axis=0, tiled=True)
    inverse_root = 1.0 / math.sqrt(float(rows * seq_count * grp_count))
    part = lax.psum_scatter(term * inverse_root, "grp", scatter_dimension=0, tiled=True)
    part = lax.all_gather(part, "seq", axis=0, tiled=False)
    per_group = width // grp_count
    wanted = jnp.arange(grp_count)
    mine = lax.axis_index("grp")
    span = HD // per_group
    outgoing = jnp.where(
        (mine // (grp_count // span) == wanted % span)[:, None, None], part[wanted // span], 0.0
    )
    incoming = lax.all_to_all(outgoing, "grp", split_axis=0, concat_axis=0, tiled=True)
    weight_grad = lax.dynamic_slice_in_dim(
        incoming, (mine % span) * (grp_count // span), grp_count // span, 0
    ).reshape(per_group, width)

    dkv = call(settle_kernel, [SMEM, VMEM, VMEM], shape(own.shape), [pltpu.VMEM(own.shape, F32)])(
        send_lists[:, :, 0], own, back
    )
    dkv = lax.all_to_all(dkv, "seq", split_axis=0, concat_axis=0, tiled=True)
    flat = shape((rows, width))
    layer_out, dq, dk, dv = call(
        unpack_kernel, [VMEM] * 3, (flat,) * 4, [pltpu.VMEM((rows, width), BF)]
    )(aq, dkv, out_weight)
    return layer_out, dq, dk, dv, weight_grad


def solution(mesh):
    nodes = P(("seq", "grp"), None)
    by_group = P("grp", None, None)
    return jax.shard_map(
        per_device,
        mesh=mesh,
        in_specs=(nodes, nodes, nodes, nodes, P(), by_group, by_group, P("grp", None)),
        out_specs=(nodes, nodes, nodes, nodes, P("grp", None)),
        check_vma=False,
    )
```

time: 616 us -> 401 us (0.65)
  waiting for transfers between devices: 332 us -> 210 us
  blocking collectives: 0 us -> 110 us
  matrix products: 102 us -> 0 us
  local copies, waits for them, and re-layouts: 68.6 us -> 13.8 us
  other arithmetic: 40.1 us -> 2.31 us
  starting transfers between devices: 55.8 us -> 26 us
  Pallas kernels: 0 us -> 22.7 us
    psum x1 -> x0, waiting for transfers between devices: 218 us -> none  [per_device(): summed = lax.psum(local_term, ('seq', 'grp'))]
    unnamed x1 -> x3, waiting for transfers between devices: 0.02 us -> 144 us
    dot_general x23 -> x0, matrix products: 88.8 us -> none  [the longest x4 28.3 us: span_step(): jnp.einsum('chij,cihe->cjhe', dscores, query_blk, preferred_element_type=...]
    all_to_all x0 -> x3, blocking collectives: none -> 88 us  [the longest x1 41.4 us: per_device(): lax.all_to_all(kv[send_lists[0, :, 0]], 'grp', split_axis=0, concat_axis=...]
    all_to_all x10 -> x4, waiting for transfers between devices: 113 us -> 66.2 us  [the longest x1 20 us: per_device(): kv = lax.all_to_all(kv, 'seq', split_axis=0, concat_axis=0, tiled=True)]
    scatter-add x5 -> x0, other arithmetic: 33 us -> none  [the longest x4 28.3 us: advance(): grad_total = grad_total.at[list_blk].add(pair_grad)]
    all_to_all x10 -> x4, starting transfers between devices: 55.8 us -> 25.9 us  [the longest x1 10.2 us: per_device(): kv = lax.all_to_all(kv, 'seq', split_axis=0, concat_axis=0, tiled=True)]
    pallas_call x0 -> x4, Pallas kernels: none -> 22.7 us  [the longest x1 17.3 us: attend(): call(attend_kernel, [SMEM, SMEM, VMEM, VMEM, VMEM], (shape((blocks, rows,...]
  transfers between devices with their start and end apart: 11 -> 6, of which waited for: 11 -> 5; matrix products, arithmetic and copies ran while one was open for 6% -> 1% of each run, Pallas kernels for 0% -> 1%
where the time goes in v1:
time: 401 us; the launch traced here: 400 us
  waiting for transfers between devices  210 us (52%)
  blocking collectives  110 us (27%)
  starting transfers between devices  26 us (6%)
  Pallas kernels  22.7 us (6%)
  between operations  14.9 us (4%)
  local copies, waits for them, and re-layouts  13.8 us (3%)
    unnamed x3, waiting for transfers between devices  144 us
    all_to_all x1, blocking collectives, per_device(): lax.all_to_all(kv[send_lists[0, :, 0]], 'grp', split_axis=0, concat_axis=...  41.4 us
    all_to_all x1, blocking collectives, per_device(): back = lax.all_to_all(halo, 'grp', split_axis=0, concat_axis=0, tiled=True)  29.8 us
    all_gather x1, blocking collectives, per_device(): part = lax.all_gather(part, 'seq', axis=0, tiled=False)  22.2 us
    all_to_all x1, waiting for transfers between devices, per_device(): kv = lax.all_to_all(kv, 'seq', split_axis=0, concat_axis=0, tiled=True)  20 us
    pallas_call x1, Pallas kernels, attend(): call(attend_kernel, [SMEM, SMEM, VMEM, VMEM, VMEM], (shape((blocks, rows,...  17.3 us
    all_to_all x1, blocking collectives, per_device(): lax.all_to_all(outgoing, 'grp', split_axis=0, concat_axis=0, tiled=True)  16.8 us
    all_to_all x1, waiting for transfers between devices, per_device(): dkv = lax.all_to_all(dkv, 'seq', split_axis=0, concat_axis=0, tiled=True)  15.9 us
  transfers between devices with their start and end apart: 6, of which 5 were waited for; matrix products, arithmetic and copies ran while one was open for 1% of the time, Pallas kernels for 1%

profile of v1, /device:TPU:1, one launch (start us, length us, event | category | flops | bytes accessed | tf_op | source)
XLA Modules:
  0.0 399.7 jit_solution(8551027704733042598)
XLA Ops:
  7.2 0.0 all-gather.4.cloned.1.call-start
  7.2 0.7 all-gather.4.cloned.1.call-update
  7.9 0.0 copy-start
  7.9 1.6 copy-done
  9.5 0.9 copy-done.3
  10.4 0.9 copy-done.8
  11.4 0.9 copy-done.9
  12.3 0.9 copy-done.10
  13.3 1.9 shard_map.119
  15.2 10.2 %all-to-all-start.1 = ((bf16[16,128,128]{2,1,0:T(8,128)(2,1)}), bf16[16,128,128]{2,1,0:T(8,128)(2,1)S(1)}, u32[]{:S(2)}, u32[]{:S(2)}) async-start(bf16[16,128,128]{2,1,0:T(8,128)(2,1)} %get-tuple-element.16), calls=%async_computation.1 | async-start | bytes 1048576 | tf_op jit(solution)/shard_map/all_to_all | solution.py:169
  25.4 0.0 copy-done.12
  25.4 20.0 %all-to-all-done.1 = bf16[16,128,128]{2,1,0:T(8,128)(2,1)S(1)} async-done(((bf16[16,128,128]{2,1,0:T(8,128)(2,1)}), bf16[16,128,128]{2,1,0:T(8,128)(2,1)S(1)}, u32[]{:S(2)}, u32[]{:S(2)}) %all-to-all-start.1) | async-done | bytes 524320 | tf_op jit(solution)/shard_map/all_to_all | solution.py:169
  45.4 0.7 gather_fusion
  46.2 0.0 copy-start.13
  46.2 41.4 %all_to_all.35 = bf16[32,128,128]{2,1,0:T(8,128)(2,1)} all-to-all(bf16[32,128,128]{2,1,0:T(8,128)(2,1)S(1)} %gather_fusion), channel_id=1, replica_groups=mesh['seq'=16,'grp'=32] {'grp'}, dimensions={0} | all-to-all | bytes 2097152 | tf_op jit(solution)/shard_map/all_to_all | solution.py:171
  87.6 4.3 %all-to-all-start = ((bf16[16,128,128]{2,1,0:T(8,128)(2,1)}), bf16[16,128,128]{2,1,0:T(8,128)(2,1)S(1)}, u32[]{:S(2)}, u32[]{:S(2)}) async-start(bf16[16,128,128]{2,1,0:T(8,128)(2,1)} %get-tuple-element.15), calls=%async_computation | async-start | bytes 1048576 | tf_op jit(solution)/shard_map/all_to_all | solution.py:170
  91.9 0.0 all-reduce.3.cloned.1.call-start
  92.0 0.0 copy-done.13
  92.0 0.1 copy.14.list_ref
  92.0 1.4 pad_maximum_fusion.kv_ref
  93.4 15.8 %all-to-all-done.qg_ref = bf16[16,128,128]{2,1,0:T(8,128)(2,1)S(1)} async-done(((bf16[16,128,128]{2,1,0:T(8,128)(2,1)}), bf16[16,128,128]{2,1,0:T(8,128)(2,1)S(1)}, u32[]{:S(2)}, u32[]{:S(2)}) %all-to-all-start) | async-done | bytes 524320 | tf_op jit(solution)/shard_map/all_to_all | solution.py:170
  109.3 0.0 copy-done.11
  109.3 17.3 %shard_map.120 = (bf16[16,128,128]{2,1,0:T(8,128)(2,1)}, f32[16,128,128]{2,1,0:T(8,128)S(1)}, bf16[32,128,128]{2,1,0:T(8,128)(2,1)S(1)}, f32[64,1024]{1,0:T(8,128)S(1)}) custom-call(s32[16,8]{1,0:T(8,128)S(1)} %copy.14.list_ref, s32[1,16]{1,0:T(1,128)S(1)} %copy-done.11, bf16[16,128,128]{2,1,0:T(8,128)(2,1)S(1)} %all-to-all-done.qg_ref, ...), custom_call_target="tpu_custom_call" | custom-call | tf_op jit(solution)/shard_map/pallas_call | solution.py:141
  126.6 0.0 copy-start.4
  126.6 1.0 copy-done.4
  127.6 1.0 copy-done.6
  128.5 0.7 broadcast_multiply_fusion
  129.3 0.0 all-reduce.3.cloned.1.call-update
  129.3 1.3 dynamic-slice
  131.3 142.9 %all-reduce.3.cloned.1.call-done = f32[64,1024]{1,0:T(8,128)} async-done(((f32[64,1024]{1,0:T(8,128)}), f32[64,1024]{1,0:T(8,128)}) %all-reduce.3.cloned.1.call-update) | async-done | bytes 262160
  274.2 0.8 dynamic-slice_bitcast_fusion
  274.9 22.2 %all-gather.1 = f32[16,2,1024]{2,1,0:T(2,128)S(1)} all-gather(f32[1,2,1024]{2,1,0:T(2,128)S(1)} %dynamic-slice_bitcast_fusion), channel_id=2, replica_groups=mesh['seq'=16,'grp'=32] {'seq'}, dimensions={0}, use_global_device_ids=true | all-gather | bytes 139264 | tf_op jit(solution)/shard_map/all_gather | solution.py:182
  297.1 0.8 gather_fusion.1
  298.0 0.2 broadcast_select_fusion
  298.1 16.8 %all_to_all.36 = f32[32,2,1024]{2,1,0:T(2,128)S(1)} all-to-all(f32[32,2,1024]{2,1,0:T(2,128)S(1)} %broadcast_select_fusion), channel_id=1, replica_groups=mesh['seq'=16,'grp'=32] {'grp'}, dimensions={0} | all-to-all | bytes 524288 | tf_op jit(solution)/shard_map/all_to_all | solution.py:190
  315.0 0.0 copy-done.7
  315.0 29.8 %all_to_all.37.back_ref = bf16[32,128,128]{2,1,0:T(8,128)(2,1)S(1)} all-to-all(bf16[32,128,128]{2,1,0:T(8,128)(2,1)S(1)} %copy-done.7), channel_id=1, replica_groups=mesh['seq'=16,'grp'=32] {'grp'}, dimensions={0} | all-to-all | bytes 2097152 | tf_op jit(solution)/shard_map/all_to_all | solution.py:179
  344.8 7.9 %all-to-all-start.3 = ((bf16[16,128,128]{2,1,0:T(8,128)(2,1)}), bf16[16,128,128]{2,1,0:T(8,128)(2,1)}, u32[]{:S(2)}, u32[]{:S(2)}) async-start(bf16[16,128,128]{2,1,0:T(8,128)(2,1)} %get-tuple-element.17), calls=%async_computation.3 | async-start | bytes 1048576 | tf_op jit(solution)/shard_map/all_to_all | solution.py:178
  352.6 1.2 copy-done.5
  353.9 0.9 shard_map.121
  354.8 0.0 copy-start.2
  354.8 0.8 copy-done.2
  355.6 14.5 %all-to-all-done.3.aq_ref = bf16[16,128,128]{2,1,0:T(8,128)(2,1)} async-done(((bf16[16,128,128]{2,1,0:T(8,128)(2,1)}), bf16[16,128,128]{2,1,0:T(8,128)(2,1)}, u32[]{:S(2)}, u32[]{:S(2)}) %all-to-all-start.3) | async-done | bytes 524320 | tf_op jit(solution)/shard_map/all_to_all | solution.py:178
  370.1 3.5 all-to-all-start.5
  373.6 0.7 reshape.94
  374.3 15.9 %all-to-all-done.5.kv_ref = bf16[16,128,128]{2,1,0:T(8,128)(2,1)S(1)} async-done(((bf16[16,128,128]{2,1,0:T(8,128)(2,1)}), bf16[16,128,128]{2,1,0:T(8,128)(2,1)S(1)}, u32[]{:S(2)}, u32[]{:S(2)}) %all-to-all-start.5) | async-done | bytes 524320 | tf_op jit(solution)/shard_map/all_to_all | solution.py:198
  390.2 0.0 copy-done.1
  390.2 2.6 shard_map.122
  (17 shorter events, 0.1 us)
Async XLA Ops:
  7.2 102.1 %all-gather.4.cloned.1.call-start = ((), (), s32[]{:S(2)}) async-start(), calls=%async_computation.7 | async-start | bytes 4456448 | tf_op jit(solution)/shard_map/all_gather | solution.py:174
  7.9 1.6 copy-start
  9.5 0.9 copy-start.3
  10.4 0.9 copy-start.8
  11.4 0.9 copy-start.9
  12.3 0.9 copy-start.10
  13.3 12.1 %copy-start.12 = (s32[1,32,1]{1,2,0:T(1,128)S(1)}, s32[1,32,1]{1,2,0:T(1,128)}, u32[]{:S(2)}) copy-start(s32[1,32,1]{1,2,0:T(1,128)} %param.13) | copy-start | bytes 388
  15.2 30.3 %all-to-all-start.1 = ((bf16[16,128,128]{2,1,0:T(8,128)(2,1)}), bf16[16,128,128]{2,1,0:T(8,128)(2,1)S(1)}, u32[]{:S(2)}, u32[]{:S(2)}) async-start(bf16[16,128,128]{2,1,0:T(8,128)(2,1)} %get-tuple-element.16), calls=%async_computation.1 | async-start | bytes 1048576 | tf_op jit(solution)/shard_map/all_to_all | solution.py:169
  46.2 45.8 %copy-start.13 = (s32[1,16,8]{1,2,0:T(8,128)S(1)}, s32[1,16,8]{1,2,0:T(8,128)}, u32[]{:S(2)}) copy-start(s32[1,16,8]{1,2,0:T(8,128)} %param.14) | copy-start | bytes 1540
  87.6 21.7 %all-to-all-start = ((bf16[16,128,128]{2,1,0:T(8,128)(2,1)}), bf16[16,128,128]{2,1,0:T(8,128)(2,1)S(1)}, u32[]{:S(2)}, u32[]{:S(2)}) async-start(bf16[16,128,128]{2,1,0:T(8,128)(2,1)} %get-tuple-element.15), calls=%async_computation | async-start | bytes 1048576 | tf_op jit(solution)/shard_map/all_to_all | solution.py:170
  91.9 182.3 %all-reduce.3.cloned.1.call-start = ((), (), s32[]{:S(2)}) async-start(), calls=%async_computation.8 | async-start | bytes 524288
  92.0 17.2 %copy-start.11 = (s32[1,16]{1,0:T(1,128)S(1)}, s32[1,16]{1,0:T(1,128)}, u32[]{:S(2)}) copy-start(s32[1,16]{1,0:T(1,128)} %count_ref.1) | copy-start | bytes 196
  126.6 1.0 copy-start.4
  127.6 1.0 copy-start.6
  128.5 186.5 %copy-start.7 = (bf16[32,128,128]{2,1,0:T(8,128)(2,1)S(1)}, bf16[32,128,128]{2,1,0:T(8,128)(2,1)}, u32[]{:S(2)}) copy-start(bf16[32,128,128]{2,1,0:T(8,128)(2,1)} %copy-done.6) | copy-start | bytes 3145732
  344.8 25.3 %all-to-all-start.3 = ((bf16[16,128,128]{2,1,0:T(8,128)(2,1)}), bf16[16,128,128]{2,1,0:T(8,128)(2,1)}, u32[]{:S(2)}, u32[]{:S(2)}) async-start(bf16[16,128,128]{2,1,0:T(8,128)(2,1)} %get-tuple-element.17), calls=%async_computation.3 | async-start | bytes 1048576 | tf_op jit(solution)/shard_map/all_to_all | solution.py:178
  352.6 1.2 copy-start.5
  353.9 36.4 %copy-start.1 = (bf16[1024,1024]{1,0:T(8,128)(2,1)S(1)}, bf16[1024,1024]{1,0:T(8,128)(2,1)}, u32[]{:S(2)}) copy-start(bf16[1024,1024]{1,0:T(8,128)(2,1)} %w_ref.3) | copy-start | bytes 6291460
  354.8 0.8 copy-start.2
  370.1 20.2 %all-to-all-start.5 = ((bf16[16,128,128]{2,1,0:T(8,128)(2,1)}), bf16[16,128,128]{2,1,0:T(8,128)(2,1)S(1)}, u32[]{:S(2)}, u32[]{:S(2)}) async-start(bf16[16,128,128]{2,1,0:T(8,128)(2,1)} %copy-done.2), calls=%async_computation.5 | async-start | bytes 1048576 | tf_op jit(solution)/shard_map/all_to_all | solution.py:198
Sparse Core Ops, SparseCore 0:
  10.1 57.5 all-gather.3
  129.4 144.7 all-reduce.2

commit v2 on v1

v2 whole, which is shorter than its diff:
```python
import functools
import math

import jax
import jax.numpy as jnp
from jax import lax
from jax.experimental import pallas as pl
from jax.experimental.pallas import tpu as pltpu
from jax.sharding import PartitionSpec as P

HD = 64
LANES = 128
BF = jnp.bfloat16
F32 = jnp.float32
VMEM = pl.BlockSpec(memory_space=pltpu.VMEM)
SMEM = pl.BlockSpec(memory_space=pltpu.SMEM)
LIMIT = 48 * 1024 * 1024
MESH = pl.DeviceIdType.MESH


def weave(left, right):
    lane = lax.broadcasted_iota(jnp.int32, left.shape, 1)
    left_f, right_f = left.astype(F32), right.astype(F32)
    first = jnp.where(lane < HD, left_f, pltpu.roll(right_f, HD, 1))
    second = jnp.where(lane < HD, pltpu.roll(left_f, HD, 1), right_f)
    return first, second


def sort_halo(send_ref, order_ref, keep_ref, last_ref, has_ref, place):
    blocks, groups = last_ref.shape[0], order_ref.shape[0]

    def clear(b, carry):
        has_ref[b] = 0
        return carry

    def count(g, carry):
        has_ref[send_ref[0, g]] += 1
        return carry

    def begin(b, at):
        place[b] = at
        after = at + has_ref[b]
        last_ref[b] = jnp.maximum(after - 1, 0)
        return after

    def put(g, carry):
        b = send_ref[0, g]
        at = place[b]
        order_ref[at] = g
        keep_ref[at] = jnp.where(at > last_ref[b] + 1 - has_ref[b], 1, 0)
        place[b] = at + 1
        return carry

    lax.fori_loop(0, blocks, clear, 0)
    lax.fori_loop(0, groups, count, 0)
    lax.fori_loop(0, blocks, begin, 0)
    lax.fori_loop(0, groups, put, 0)


def attend_kernel(
    send_ref,
    list_ref,
    count_ref,
    qg_ref,
    own_kv,
    halo_kv,
    aq_ref,
    own_ref,
    halo_ref,
    att_t,
    order_ref,
    keep_ref,
    last_ref,
    has_ref,
    kv_ref,
    kv_t,
    acc,
    place,
):
    blocks, rows, _ = qg_ref.shape
    space = kv_ref.shape[0]
    listed = list_ref.shape[1]
    scale = 1.0 / math.sqrt(HD)

    def prepare(part, base):
        def step(i, carry):
            block = part[i]
            kv_ref[base + i] = block
            kv_t[base + i] = block.T
            acc[base + i] = jnp.zeros(acc.shape[1:], F32)
            return carry

        lax.fori_loop(0, part.shape[0], step, 0, unroll=4)

    prepare(own_kv, 0)
    prepare(halo_kv, blocks)
    sort_halo(send_ref, order_ref, keep_ref, last_ref, has_ref, place)

    def one(b, live):
        qg = qg_ref[b]
        lane = lax.broadcasted_iota(jnp.int32, qg.shape, 1)
        full = qg.astype(F32)
        x = jnp.concatenate(
            (
                jnp.where(lane < HD, full * scale, 0.0).astype(BF),
                jnp.where(lane < HD, 0.0, full).astype(BF),
            ),
            axis=0,
        )
        index = [list_ref[b, t] for t in range(live)]
        keys = jnp.concatenate([kv_ref[i] for i in index], axis=0)
        both = lax.dot_general(keys, x, (((1,), (1,)), ((), ())), preferred_element_type=F32)
        scores, dprobs = both[:, :rows], both[:, rows:]
        weights = jnp.exp(scores - jnp.max(scores, axis=0, keepdims=True))
        inverse = 1.0 / jnp.sum(weights, axis=0, keepdims=True)
        probs = weights * inverse
        inner = jnp.sum(probs * dprobs, axis=0, keepdims=True)
        z = jnp.concatenate((probs * (dprobs - inner), probs), axis=1).astype(BF)
        pair = jnp.dot(z, x, preferred_element_type=F32)
        for t, i in enumerate(index):
            acc[i] += pair[t * rows : (t + 1) * rows]
        turned = jnp.concatenate([kv_t[i] for i in index], axis=1)
        out = jnp.dot(turned, z, preferred_element_type=F32)
        attended = out[HD:, rows:]
        att_t[:, pl.ds(pl.multiple_of(b * rows, rows), rows)] = attended.astype(BF)
        aq_ref[b] = jnp.concatenate((out[:HD, :rows] * scale, attended), axis=0).T.astype(BF)

    def step(b, carry):
        count = count_ref[0, b]
        for live in range(1, listed + 1):
            pl.when(count == live)(functools.partial(one, b, live))
        return carry

    lax.fori_loop(0, blocks, step, 0)
    own_ref[...] = acc[:blocks]
    halo_ref[...] = acc[blocks:].astype(BF)


def unpack_kernel(aq_ref, kv_ref, w_ref, out_ref, dq_ref, dk_ref, dv_ref, att):
    for j in range(aq_ref.shape[0] // 2):
        cols = slice(j * LANES, (j + 1) * LANES)
        first, second = weave(aq_ref[2 * j], aq_ref[2 * j + 1])
        dq_ref[:, cols] = first.astype(BF)
        att[:, cols] = second.astype(BF)
        first, second = weave(kv_ref[2 * j], kv_ref[2 * j + 1])
        dk_ref[:, cols] = first.astype(BF)
        dv_ref[:, cols] = second.astype(BF)
    out_ref[...] = jnp.dot(att[...], w_ref[...], preferred_element_type=F32).astype(BF)


def shape(dims, kind=BF):
    return jax.ShapeDtypeStruct(dims, kind)


def call(kernel, in_specs, out_shape, scratch=(), **kw):
    return pl.pallas_call(
        kernel,
        in_specs=in_specs,
        out_specs=jax.tree.map(lambda _: VMEM, out_shape),
        out_shape=out_shape,
        scratch_shapes=list(scratch),
        compiler_params=pltpu.CompilerParams(vmem_limit_bytes=LIMIT),
        **kw,
    )


def attend(send, lists, counts, qg, own_kv, halo_kv):
    blocks, rows, lanes = qg.shape
    groups = halo_kv.shape[0]
    space = blocks + groups
    ints = [shape((n,), jnp.int32) for n in (groups, groups, blocks, blocks)]
    return pl.pallas_call(
        attend_kernel,
        in_specs=[SMEM] * 3 + [VMEM] * 3,
        out_specs=(VMEM,) * 4 + (SMEM,) * 4,
        out_shape=(
            shape((blocks, rows, lanes)),
            shape((blocks, rows, lanes), F32),
            shape((groups, rows, lanes)),
            shape((HD, blocks * rows)),
            *ints,
        ),
        scratch_shapes=[
            pltpu.VMEM((space, rows, lanes), BF),
            pltpu.VMEM((space, lanes, rows), BF),
            pltpu.VMEM((space, rows, lanes), F32),
            pltpu.SMEM((blocks,), jnp.int32),
        ],
        compiler_params=pltpu.CompilerParams(vmem_limit_bytes=LIMIT),
    )(send, lists, counts, qg, own_kv, halo_kv)


def signal(semaphore, seq, grp):
    pl.semaphore_signal(semaphore, inc=1, device_id=(seq, grp), device_id_type=MESH)


def others(count, body):
    def step(k, carry):
        body(k)
        return carry

    lax.fori_loop(1, count, step, 0)


def push(src, dst, send, recv, seq, grp):
    return pltpu.make_async_remote_copy(
        src_ref=src,
        dst_ref=dst,
        send_sem=send,
        recv_sem=recv,
        device_id=(seq, grp),
        device_id_type=MESH,
    )


def bring_kernel(
    send_ref,
    q_ref,
    k_ref,
    v_ref,
    c_ref,
    w_hbm,
    kv_ref,
    halo_ref,
    qg_ref,
    kv_out,
    qg_out,
    halo_out,
    w_ref,
    w_sem,
    kv_send,
    kv_recv,
    qg_send,
    qg_recv,
    halo_send,
    halo_recv,
):
    seq, grp = lax.axis_index("seq"), lax.axis_index("grp")
    n_seq, n_grp = kv_ref.shape[0], halo_ref.shape[0]
    load_w = pltpu.make_async_copy(w_hbm, w_ref, w_sem)
    load_w.start()
    barrier = pltpu.get_barrier_semaphore()
    others(n_seq, lambda k: signal(barrier, lax.rem(seq + k, n_seq), grp))
    others(n_grp, lambda k: signal(barrier, seq, lax.rem(grp + k, n_grp)))

    tiles = [slice(j * LANES, (j + 1) * LANES) for j in range(n_seq // 2)]
    for j, cols in enumerate(tiles):
        first, second = weave(k_ref[:, cols], v_ref[:, cols])
        kv_out[2 * j] = first.astype(BF)
        kv_out[2 * j + 1] = second.astype(BF)
    pl.semaphore_wait(barrier, n_seq + n_grp - 2)

    def kv_copy(k):
        to = lax.rem(seq + k, n_seq)
        return push(kv_out.at[to], kv_ref.at[seq], kv_send.at[k], kv_recv.at[k], to, grp)

    def qg_copy(k):
        to = lax.rem(seq + k, n_seq)
        return push(qg_out.at[to], qg_ref.at[seq], qg_send.at[k], qg_recv.at[k], to, grp)

    def halo_copy(k):
        to = lax.rem(grp + k, n_grp)
        return push(halo_out.at[to], halo_ref.at[grp], halo_send.at[k], halo_recv.at[k], seq, to)

    others(n_seq, lambda k: kv_copy(k).start())
    load_w.wait()
    grad = lax.dot_general(
        c_ref[...], w_ref[...], (((1,), (1,)), ((), ())), preferred_element_type=F32
    ).astype(BF)
    for j, cols in enumerate(tiles):
        first, second = weave(q_ref[:, cols], grad[:, cols])
        qg_out[2 * j] = first.astype(BF)
        qg_out[2 * j + 1] = second.astype(BF)
    others(n_seq, lambda k: qg_copy(k).start())
    kv_ref[seq] = kv_out[seq]
    qg_ref[seq] = qg_out[seq]
    others(n_seq, lambda k: kv_copy(k).wait_recv())

    def forward(k):
        to = lax.rem(grp + k, n_grp)
        halo_out[to] = kv_ref[send_ref[0, to]]
        halo_copy(k).start()

    others(n_grp, forward)
    halo_ref[grp] = kv_ref[send_ref[0, grp]]
    others(n_seq, lambda k: qg_copy(k).wait_recv())
    others(n_grp, lambda k: halo_copy(k).wait_recv())
    others(n_seq, lambda k: kv_copy(k).wait_send())
    others(n_seq, lambda k: qg_copy(k).wait_send())
    others(n_grp, lambda k: halo_copy(k).wait_send())


def bring(send, q, k, v, cot, weight, n_seq, n_grp):
    tile = (q.shape[0], LANES)
    return pl.pallas_call(
        bring_kernel,
        in_specs=[SMEM, VMEM, VMEM, VMEM, VMEM, pl.BlockSpec(memory_space=pl.ANY)],
        out_specs=(VMEM,) * 3,
        out_shape=(shape((n_seq,) + tile), shape((n_grp,) + tile), shape((n_seq,) + tile)),
        scratch_shapes=[
            pltpu.VMEM((n_seq,) + tile, BF),
            pltpu.VMEM((n_seq,) + tile, BF),
            pltpu.VMEM((n_grp,) + tile, BF),
            pltpu.VMEM(weight.shape, BF),
            pltpu.SemaphoreType.DMA,
        ]
        + [pltpu.SemaphoreType.DMA((n,)) for n in (n_seq,) * 4 + (n_grp,) * 2],
        compiler_params=pltpu.CompilerParams(
            vmem_limit_bytes=LIMIT, collective_id=0, has_side_effects=True
        ),
    )(send, q, k, v, cot, weight)


def return_kernel(
    inverse_root,
    order_ref,
    keep_ref,
    last_ref,
    has_ref,
    aq_ref,
    own_ref,
    halo_ref,
    att_ref,
    cot_hbm,
    aq_out,
    kv_out,
    wg_out,
    cot_ref,
    back,
    running,
    dkv,
    term,
    parts,
    share,
    cot_sem,
    aq_send,
    aq_recv,
    kv_send,
    kv_recv,
    halo_send,
    halo_recv,
    part_send,
    part_recv,
    wg_send,
    wg_recv,
):
    seq, grp = lax.axis_index("seq"), lax.axis_index("grp")
    n_seq, n_grp = aq_ref.shape[0], halo_ref.shape[0]
    half = wg_out.shape[0] // 2
    load_cot = pltpu.make_async_copy(cot_hbm, cot_ref, cot_sem)
    load_cot.start()
    barrier = pltpu.get_barrier_semaphore()
    others(n_seq, lambda k: signal(barrier, lax.rem(seq + k, n_seq), grp))
    others(n_grp, lambda k: signal(barrier, seq, lax.rem(grp + k, n_grp)))
    source = grp // 2

    def greet(g, carry):
        @pl.when((source != seq) | (g != grp))
        def _():
            signal(barrier, source, g)

        return carry

    lax.fori_loop(0, n_grp, greet, 0)
    keeps_one = grp // 2 == seq
    pl.semaphore_wait(barrier, n_seq + n_grp - 2 + 2 * n_seq - jnp.where(keeps_one, 1, 0))

    def aq_copy(k):
        to = lax.rem(seq + k, n_seq)
        return push(aq_ref.at[to], aq_out.at[seq], aq_send.at[k], aq_recv.at[k], to, grp)

    def kv_copy(k):
        to = lax.rem(seq + k, n_seq)
        return push(dkv.at[to], kv_out.at[seq], kv_send.at[k], kv_recv.at[k], to, grp)

    def halo_copy(k):
        to = lax.rem(grp + k, n_grp)
        return push(halo_ref.at[to], back.at[grp], halo_send.at[k], halo_recv.at[k], seq, to)

    def corner(piece):
        return (
            pl.ds(pl.multiple_of((piece % 2) * half, half), half),
            pl.ds(pl.multiple_of((piece // 2) * LANES, LANES), LANES),
        )

    def part_copy(row, piece):
        rows, cols = corner(piece)
        return push(
            term.at[row, rows, cols],
            parts.at[grp],
            part_send.at[row, piece],
            part_recv.at[grp],
            piece,
            2 * seq + row,
        )

    def wg_copy(k):
        to = lax.rem(seq + k, n_seq)
        return push(share, wg_out.at[corner(seq)], wg_send.at[k], wg_recv.at[k], to, grp)

    def wg_arrival(k):
        come = lax.rem(seq + n_seq - k, n_seq)
        return push(share, wg_out.at[corner(come)], wg_send.at[k], wg_recv.at[k], come, grp)

    others(n_grp, lambda k: halo_copy(k).start())
    others(n_seq, lambda k: aq_copy(k).start())
    aq_out[seq] = aq_ref[seq]
    back[grp] = halo_ref[grp]

    load_cot.wait()
    total = jnp.dot(att_ref[...], cot_ref[...], preferred_element_type=F32) * inverse_root
    term[0] = total[: 2 * half]
    term[1] = total[2 * half :]

    def elsewhere(row, piece):
        return (piece != seq) | (2 * seq + row != grp)

    def each_part(body):
        for row in range(2):

            def step(piece, carry, row=row):
                pl.when(elsewhere(row, piece))(lambda: body(row, piece))
                return carry

            lax.fori_loop(0, n_seq, step, 0)

    each_part(lambda row, piece: part_copy(row, piece).start())

    @pl.when(keeps_one)
    def _():
        rows, cols = corner(seq)
        parts[grp] = term[grp % 2, rows, cols]

    def part_wait(g, carry):
        @pl.when((source != seq) | (g != grp))
        def _():
            push(
                term.at[0, :half, :LANES],
                parts.at[g],
                part_send.at[0, 0],
                part_recv.at[g],
                source,
                g,
            ).wait_recv()

        return carry

    lax.fori_loop(0, n_grp, part_wait, 0)
    share[...] = jnp.sum(parts[...], axis=0)
    others(n_seq, lambda k: wg_copy(k).start())
    rows, cols = corner(seq)
    wg_out[rows, cols] = share[...]

    others(n_grp, lambda k: halo_copy(k).wait_recv())

    def run(j, total):
        total = jnp.where(keep_ref[j] != 0, total, 0.0) + back[order_ref[j]].astype(F32)
        running[j] = total
        return total

    lax.fori_loop(0, n_grp, run, jnp.zeros(running.shape[1:], F32))

    def settle(b, carry):
        more = jnp.where(has_ref[b] != 0, running[last_ref[b]], 0.0)
        dkv[b] = (own_ref[b] + more).astype(BF)
        return carry

    lax.fori_loop(0, n_seq, settle, 0)
    others(n_seq, lambda k: kv_copy(k).start())
    kv_out[seq] = dkv[seq]

    others(n_seq, lambda k: aq_copy(k).wait_recv())
    others(n_seq, lambda k: wg_arrival(k).wait_recv())
    others(n_seq, lambda k: kv_copy(k).wait_recv())
    others(n_grp, lambda k: halo_copy(k).wait_send())
    others(n_seq, lambda k: aq_copy(k).wait_send())
    each_part(lambda row, piece: part_copy(row, piece).wait_send())
    others(n_seq, lambda k: wg_copy(k).wait_send())
    others(n_seq, lambda k: kv_copy(k).wait_send())


def bring_back(lists, aq, own, halo, att, cot, inverse_root):
    n_seq, n_grp = aq.shape[0], halo.shape[0]
    tile = aq.shape[1:]
    width = cot.shape[1]
    per_group = width // n_grp
    return pl.pallas_call(
        functools.partial(return_kernel, inverse_root),
        in_specs=[SMEM] * 4 + [VMEM] * 4 + [pl.BlockSpec(memory_space=pl.ANY)],
        out_specs=(VMEM,) * 3,
        out_shape=(shape(aq.shape), shape(aq.shape), shape((per_group, width), F32)),
        scratch_shapes=[
            pltpu.VMEM(cot.shape, BF),
            pltpu.VMEM(halo.shape, BF),
            pltpu.VMEM((n_grp,) + tile, F32),
            pltpu.VMEM(aq.shape, BF),
            pltpu.VMEM((2, per_group, width), F32),
            pltpu.VMEM((n_grp, per_group // 2, LANES), F32),
            pltpu.VMEM((per_group // 2, LANES), F32),
            pltpu.SemaphoreType.DMA,
        ]
        + [pltpu.SemaphoreType.DMA((n,)) for n in (n_seq,) * 4 + (n_grp,) * 2]
        + [
            pltpu.SemaphoreType.DMA((2, n_seq)),
            pltpu.SemaphoreType.DMA((n_grp,)),
            pltpu.SemaphoreType.DMA((n_seq,)),
            pltpu.SemaphoreType.DMA((n_seq,)),
        ],
        compiler_params=pltpu.CompilerParams(
            vmem_limit_bytes=LIMIT, collective_id=1, has_side_effects=True
        ),
    )(*lists, aq, own, halo, att, cot)


def per_device(
    queries, key_rows, value_rows, cotangent, out_weight, send_lists, key_blocks, key_counts
):
    n_seq = lax.axis_size("seq")
    n_grp = lax.axis_size("grp")
    rows, width = queries.shape
    send = send_lists[:, :, 0]
    kv, halo, qg = bring(
        send, queries, key_rows, value_rows, cotangent, out_weight, n_seq, n_grp
    )
    cot = lax.all_gather(cotangent, "seq", axis=0, tiled=True)
    aq, own, halo, att, *lists = attend(send, key_blocks[0], key_counts, qg, kv, halo)
    inverse_root = 1.0 / math.sqrt(float(rows * n_seq * n_grp))
    aq, dkv, weight_grad = bring_back(lists, aq, own, halo, att, cot, inverse_root)
    flat = shape((rows, width))
    layer_out, dq, dk, dv = call(
        unpack_kernel, [VMEM] * 3, (flat,) * 4, [pltpu.VMEM((rows, width), BF)]
    )(aq, dkv, out_weight)
    return layer_out, dq, dk, dv, weight_grad


def solution(mesh):
    nodes = P(("seq", "grp"), None)
    by_group = P("grp", None, None)
    return jax.shard_map(
        per_device,
        mesh=mesh,
        in_specs=(nodes, nodes, nodes, nodes, P(), by_group, by_group, P("grp", None)),
        out_specs=(nodes, nodes, nodes, nodes, P("grp", None)),
        check_vma=False,
    )
```

time: 401 us -> 166 us (0.41)
  waiting for transfers between devices: 210 us -> 0.68 us
  Pallas kernels: 22.7 us -> 138 us
  blocking collectives: 110 us -> 0 us
  starting transfers between devices: 26 us -> 0.04 us
    unnamed x3 -> x1, waiting for transfers between devices: 144 us -> 0.68 us
    pallas_call x3, Pallas kernels: 20 us -> 136 us  [the longest x1 63.3 us: bring(): pl.pallas_call(bring_kernel, in_specs=[SMEM, VMEM, VMEM, VMEM, VMEM, pl.B...]
    all_to_all x3 -> x0, blocking collectives: 88 us -> none  [the longest x1 41.4 us: per_device(): lax.all_to_all(kv[send_lists[0, :, 0]], 'grp', split_axis=0, concat_axis=...]
    all_to_all x4 -> x0, waiting for transfers between devices: 66.2 us -> none  [the longest x1 20 us: per_device(): kv = lax.all_to_all(kv, 'seq', split_axis=0, concat_axis=0, tiled=True)]
    all_to_all x4 -> x0, starting transfers between devices: 25.9 us -> none  [the longest x1 10.2 us: per_device(): kv = lax.all_to_all(kv, 'seq', split_axis=0, concat_axis=0, tiled=True)]
    all_gather x1 -> x0, blocking collectives: 22.2 us -> none  [per_device(): part = lax.all_gather(part, 'seq', axis=0, tiled=False)]
    unnamed x30 -> x25, local copies, waits for them, and re-layouts: 11.4 us -> 11.4 us
  transfers between devices with their start and end apart: 6 -> 1, of which waited for: 5 -> 0; matrix products, arithmetic and copies ran while one was open for 1% -> 0% of each run, Pallas kernels for 1% -> 48%
where the time goes in v2:
time: 166 us; the launch traced here: 165 us
  Pallas kernels  138 us (83%)
  between operations  14.1 us (8%)
  local copies, waits for them, and re-layouts  12.2 us (7%)
    pallas_call x1, Pallas kernels, bring(): pl.pallas_call(bring_kernel, in_specs=[SMEM, VMEM, VMEM, VMEM, VMEM, pl.B...  63.3 us
    pallas_call x1, Pallas kernels, bring_back(): pl.pallas_call(functools.partial(return_kernel, inverse_root), in_specs=[...  57 us
    pallas_call x1, Pallas kernels, attend(): pl.pallas_call(attend_kernel, in_specs=[SMEM] * 3 + [VMEM] * 3, out_specs...  16 us
    unnamed x25, local copies, waits for them, and re-layouts  11.4 us
  transfers between devices with their start and end apart: 1, of which 0 were waited for; matrix products, arithmetic and copies ran while one was open for 0% of the time, Pallas kernels for 48%

profile of v2, /device:TPU:1, one launch (start us, length us, event | category | flops | bytes accessed | tf_op | source)
XLA Modules:
  0.0 164.9 jit_solution(2969470650962842593)
XLA Ops:
  7.2 0.0 all-gather.2.cloned.1.call-start
  7.2 0.7 all-gather.2.cloned.1.call-update
  7.9 0.8 copy.13.list_ref
  8.7 0.0 copy-start
  8.7 1.6 copy-done
  10.2 0.0 copy-start.4
  10.3 0.9 copy-done.4
  11.2 0.0 copy-start.7
  11.2 0.9 copy-done.7
  12.2 0.0 copy-start.8
  12.2 0.9 copy-done.8
  13.1 0.0 copy-start.9
  13.1 0.9 copy-done.9
  14.1 0.0 copy-start.10
  14.1 0.7 copy-done.10
  14.7 63.3 %shard_map.119 = (bf16[16,128,128]{2,1,0:T(8,128)(2,1)S(1)}, bf16[32,128,128]{2,1,0:T(8,128)(2,1)S(1)}, bf16[16,128,128]{2,1,0:T(8,128)(2,1)S(1)}) custom-call(s32[1,32]{1,0:T(1,128)S(1)} %bitcast.2, bf16[128,1024]{1,0:T(8,128)(2,1)S(1)} %copy-done.7, bf16[128,1024]{1,0:T(8,128)(2,1)S(1)} %copy-done.8, bf16[128,1024]{1,0:T(8,128)(2,1)S(1)} %copy-done.9, ...), custom_call_target="tpu_custom_call" | custom-call | tf_op jit(solution)/shard_map/pallas_call | solution.py:295
  78.0 0.0 copy-start.11
  78.0 0.6 copy-done.11
  78.7 0.0 copy-start.1
  78.7 16.0 %shard_map.120 = (bf16[16,128,128]{2,1,0:T(8,128)(2,1)S(1)}, f32[16,128,128]{2,1,0:T(8,128)S(1)}, bf16[32,128,128]{2,1,0:T(8,128)(2,1)S(1)}, bf16[64,2048]{1,0:T...) custom-call(s32[1,32]{1,0:T(1,128)S(1)} %bitcast.3, ...), custom_call_target="tpu_custom_call" | custom-call | tf_op jit(solution)/shard_map/pallas_call | solution.py:172
  94.7 0.0 copy-start.2
  94.7 1.0 copy-done.2
  95.7 0.0 copy-start.5
  95.7 0.8 copy-done.5
  96.5 0.0 all-gather.2.cloned.1.call-done.cot_hbm
  96.5 0.0 copy-start.3
  96.5 1.2 copy-done.3
  97.7 0.0 copy-start.6
  97.8 1.0 copy-done.6
  98.8 57.0 %shard_map.121 = (bf16[16,128,128]{2,1,0:T(8,128)(2,1)S(1)}, bf16[16,128,128]{2,1,0:T(8,128)(2,1)S(1)}, f32[32,1024]{1,0:T(8,128)S(1)}) custom-call(s32[32]{0:T(128)S(1)} %get-tuple-element.26.order_ref, s32[32]{0:T(128)S(1)} %get-tuple-element.27.keep_ref, s32[16]{0:T(128)S(1)} %get-tuple-element.28.last_ref, s32[16]{0:T(128)S(1)} %get-tuple-element.29.has_ref, ...), custom_call_target="tpu_custom_call" | custom-call | tf_op jit(solution)/shard_map/pallas_call | solution.py:487
  155.8 0.0 copy-done.1
  155.8 1.6 shard_map.122
  157.4 0.7 copy.15
Async XLA Ops:
  7.2 89.4 %all-gather.2.cloned.1.call-start = ((), (), s32[]{:S(2)}) async-start(), calls=%async_computation | async-start | bytes 4456448 | tf_op jit(solution)/shard_map/all_gather | solution.py:525
  8.7 1.6 copy-start
  10.2 0.9 copy-start.4
  11.2 0.9 copy-start.7
  12.2 0.9 copy-start.8
  13.1 0.9 copy-start.9
  14.1 0.7 copy-start.10
  78.0 0.7 copy-start.11
  78.7 77.1 %copy-start.1 = (bf16[1024,1024]{1,0:T(8,128)(2,1)S(1)}, bf16[1024,1024]{1,0:T(8,128)(2,1)}, u32[]{:S(2)}) copy-start(bf16[1024,1024]{1,0:T(8,128)(2,1)} %w_ref.1) | copy-start | bytes 6291460
  94.7 1.0 copy-start.2
  95.7 0.8 copy-start.5
  96.5 1.2 copy-start.3
  97.7 1.0 copy-start.6
Sparse Core Ops, SparseCore 0:
  10.1 69.7 all-gather.1

commit v3 on v1

v3 whole, which is shorter than its diff:
```python
import functools
import math

import jax
import jax.numpy as jnp
from jax import lax
from jax.experimental import pallas as pl
from jax.experimental.pallas import tpu as pltpu
from jax.sharding import PartitionSpec as P

HD = 64
LANES = 128
BF = jnp.bfloat16
F32 = jnp.float32
VMEM = pl.BlockSpec(memory_space=pltpu.VMEM)
SMEM = pl.BlockSpec(memory_space=pltpu.SMEM)
ANY = pl.BlockSpec(memory_space=pl.ANY)
LIMIT = 60 * 1024 * 1024
CHUNKS = 2
MESH = pl.DeviceIdType.MESH


def weave(left, right):
    lane = lax.broadcasted_iota(jnp.int32, left.shape, 1)
    left_f, right_f = left.astype(F32), right.astype(F32)
    first = jnp.where(lane < HD, left_f, pltpu.roll(right_f, HD, 1))
    second = jnp.where(lane < HD, pltpu.roll(left_f, HD, 1), right_f)
    return first, second


def shape(dims, kind=BF):
    return jax.ShapeDtypeStruct(dims, kind)


def signal(semaphore, seq, grp):
    pl.semaphore_signal(semaphore, inc=1, device_id=(seq, grp), device_id_type=MESH)


def others(count, body):
    def step(k, carry):
        body(k)
        return carry

    lax.fori_loop(1, count, step, 0)


def each(count, body, unroll=1):
    def step(i, carry):
        body(i)
        return carry

    lax.fori_loop(0, count, step, 0, unroll=unroll)


def push(src, dst, send, recv, seq, grp):
    return pltpu.make_async_remote_copy(
        src_ref=src,
        dst_ref=dst,
        send_sem=send,
        recv_sem=recv,
        device_id=(seq, grp),
        device_id_type=MESH,
    )


def local(src, dst, semaphore):
    return pltpu.make_async_copy(src, dst, semaphore)


def rows_of(ref, block, chunk):
    rows = ref.shape[1] // CHUNKS
    return ref.at[block, pl.ds(chunk * rows, rows)]


def place_order(place):
    row = lax.broadcasted_iota(jnp.int32, place.shape, 0).astype(F32)
    col = lax.broadcasted_iota(jnp.int32, place.shape, 1).astype(F32)
    other = place.T
    earlier = (other < place) | ((other == place) & (col < row))
    rank = jnp.sum(jnp.where(earlier, 1.0, 0.0), axis=1, keepdims=True)
    there = rank == col

    def down(mask, value):
        return jnp.sum(jnp.where(mask, value, 0.0), axis=0, keepdims=True)

    order = down(there, row)
    sorted_place = down(there, place)
    again = (sorted_place == pltpu.roll(sorted_place, 1, 1)) & (col[:1] > 0.0)
    last = jnp.maximum(down(place <= col, 1.0) - 1.0, 0.0)
    return jnp.concatenate(
        (order, jnp.where(again, 1.0, 0.0), last, down(place == col, 1.0)), axis=0
    ).astype(jnp.int32)


def plan_kernel(send_ref, list_ref, plan_ref, place):
    listed, blocks = list_ref.shape[1:]
    groups = send_ref.shape[2]

    def put(i, value):
        place[pl.ds(i, 1), :] = jnp.full((1, place.shape[1]), value, jnp.int32)

    def pairs(b):
        for t in range(listed):
            put(b * listed + t, list_ref[0, t, b])

    each(blocks, pairs)
    for_pairs = place_order(place[...].astype(F32))
    place[...] = jnp.full(place.shape, place.shape[1], jnp.int32)
    each(groups, lambda g: put(g, send_ref[0, 0, g]))
    plan_ref[...] = jnp.concatenate((for_pairs, place_order(place[...].astype(F32))), axis=0)


def make_plan(send, lists):
    items = lists.shape[1] * lists.shape[2]
    return pl.pallas_call(
        plan_kernel,
        in_specs=[SMEM] * 2,
        out_specs=VMEM,
        out_shape=shape((8, items), jnp.int32),
        scratch_shapes=[pltpu.VMEM((items, items), jnp.int32)],
    )(send, lists)


def split_pair(pair):
    lane = lax.broadcasted_iota(jnp.int32, pair.shape, 1)
    full = pair.astype(F32)
    scale = 1.0 / math.sqrt(HD)
    return jnp.concatenate(
        (
            jnp.where(lane < HD, full * scale, 0.0).astype(BF),
            jnp.where(lane < HD, 0.0, full).astype(BF),
        ),
        axis=0,
    )


def attend_blocks(blocks, list_ref, count_ref, x_ref, kv_ref, kv_t, aq_ref, att_t, terms):
    listed = list_ref.shape[1]
    rows = kv_ref.shape[1]
    scale = 1.0 / math.sqrt(HD)
    span = range(listed)
    index = [[list_ref[0, t, b] for t in span] for b in blocks]
    xs = [x_ref[b] for b in blocks]
    both = [
        lax.dot_general(
            jnp.concatenate([kv_ref[i] for i in at], axis=0),
            x,
            (((1,), (1,)), ((), ())),
            preferred_element_type=F32,
        )
        for at, x in zip(index, xs)
    ]
    zs = []
    for b, pair in zip(blocks, both):
        bias = [jnp.where(count_ref[0, b] > t, 0.0, -jnp.inf).astype(F32) for t in span]
        scores = [pair[t * rows : (t + 1) * rows, :rows] + bias[t] for t in span]
        dprobs = [pair[t * rows : (t + 1) * rows, rows:] for t in span]
        top = functools.reduce(jnp.maximum, scores)
        top = jnp.max(top, axis=0, keepdims=True)
        weights = [jnp.exp(s - top) for s in scores]
        inverse = 1.0 / jnp.sum(sum(weights), axis=0, keepdims=True)
        inner = sum(w * d for w, d in zip(weights, dprobs))
        inner = jnp.sum(inner, axis=0, keepdims=True) * inverse
        z = []
        for w, d in zip(weights, dprobs):
            probs = w * inverse
            z.append(jnp.concatenate((probs * (d - inner), probs), axis=1).astype(BF))
        zs.append(z)
    for b, z, x in zip(blocks, zs, xs):
        pair = jnp.dot(jnp.concatenate(z, axis=0), x, preferred_element_type=F32)
        for t in span:
            terms[b * listed + t] = pair[t * rows : (t + 1) * rows]
    for b, z, at in zip(blocks, zs, index):
        turned = jnp.concatenate([kv_t[i] for i in at], axis=1)
        out = jnp.dot(turned, jnp.concatenate(z, axis=0), preferred_element_type=F32)
        attended = out[HD:, rows:]
        att_t[b] = attended.astype(BF)
        aq_ref[b] = jnp.concatenate((out[:HD, :rows] * scale, attended), axis=0).T.astype(BF)


def sums_by_place(plan_ref, at, source, running):
    def run(j, total):
        total = jnp.where(plan_ref[at + 1, j] != 0, total, 0.0)
        total = total + source[plan_ref[at, j]].astype(F32)
        running[j] = total
        return total

    lax.fori_loop(0, running.shape[0], run, jnp.zeros(running.shape[1:], F32), unroll=4)


def sum_of(place, plan_ref, at, running):
    return jnp.where(plan_ref[at + 3, place] != 0, running[plan_ref[at + 2, place]], 0.0)


OFFSETS = (0, -1, 1, -2, 2, -3, 3, 4)
SIDE = 4


def layer_kernel(
    inverse_root,
    send_ref,
    list_ref,
    count_ref,
    plan_ref,
    q_hbm,
    k_hbm,
    v_hbm,
    c_hbm,
    w_hbm,
    out_hbm,
    dq_hbm,
    kv_back,
    wg_out,
    q_ref,
    k_ref,
    v_ref,
    c_ref,
    w_ref,
    kv_out,
    kv_in,
    qg_out,
    qg_in,
    halo_out,
    kv_ref,
    kv_t,
    x_ref,
    terms,
    running,
    aq_out,
    aq_in,
    att_t,
    att_n,
    own_grad,
    halo_grad,
    back,
    back_sum,
    dkv,
    cot_ref,
    total,
    term,
    parts,
    share,
    load_sem,
    local_sem,
    ring_send,
    ring_recv,
    core_send,
    core_recv,
    kv_send,
    kv_recv,
    qg_send,
    qg_recv,
    halo_send,
    halo_recv,
    aq_send,
    aq_recv,
    hg_send,
    hg_recv,
    dkv_send,
    dkv_recv,
    part_send,
    part_recv,
    wg_send,
    wg_recv,
):
    seq, grp = lax.axis_index("seq"), lax.axis_index("grp")
    n_seq, n_grp = qg_in.shape[0], halo_grad.shape[0]
    size = kv_in[0].shape[1]
    half = wg_out.shape[0] // 2
    middle = cot_ref.shape[2] // 2
    right, left = lax.rem(seq + 2, n_seq), lax.rem(seq + n_seq - 2, n_seq)
    core = lax.rem(seq, 2)
    sibling = seq + 1 - 2 * core
    source = grp // 2
    keeps_one = source == seq
    tiles = [slice(j * LANES, (j + 1) * LANES) for j in range(n_seq // 2)]

    pairs = ((k_hbm, k_ref), (v_hbm, v_ref), (c_hbm, c_ref), (w_hbm, w_ref), (q_hbm, q_ref))
    loads = [local(src, dst, load_sem.at[i]) for i, (src, dst) in enumerate(pairs)]
    for load in loads:
        load.start()
    barrier = pltpu.get_barrier_semaphore()
    others(n_seq, lambda k: signal(barrier, lax.rem(seq + k, n_seq), grp))
    others(n_grp, lambda k: signal(barrier, seq, lax.rem(grp + k, n_grp)))

    def from_source(g, body):
        pl.when((source != seq) | (g != grp))(body)

    each(n_grp, lambda g: from_source(g, lambda: signal(barrier, source, g)))

    def kv_copy(c, k):
        to = lax.rem(seq + k, n_seq)
        return push(
            rows_of(kv_out, to, c), kv_in[c].at[seq], kv_send.at[c, k], kv_recv.at[c, k], to, grp
        )

    def qg_copy(k):
        to = lax.rem(seq + k, n_seq)
        return push(qg_out.at[to], qg_in.at[seq], qg_send.at[k], qg_recv.at[k], to, grp)

    def halo_copy(c, k):
        to = lax.rem(grp + k, n_grp)
        return push(
            halo_out.at[c, to],
            rows_of(kv_ref, n_seq + grp, c),
            halo_send.at[c, k],
            halo_recv.at[c, k],
            seq,
            to,
        )

    def halo_arrival(c, k):
        come = lax.rem(grp + n_grp - k, n_grp)
        return push(
            halo_out.at[c, come],
            rows_of(kv_ref, n_seq + come, c),
            halo_send.at[c, k],
            halo_recv.at[c, k],
            seq,
            come,
        )

    def aq_copy(b):
        return push(aq_out.at[b], aq_in.at[seq], aq_send.at[b], aq_recv.at[seq], b, grp)

    def aq_arrival(b):
        return push(aq_out.at[b], aq_in.at[b], aq_send.at[b], aq_recv.at[b], b, grp)

    def hg_copy(c, k):
        to = lax.rem(grp + k, n_grp)
        return push(
            rows_of(halo_grad, to, c), back[c].at[grp], hg_send.at[c, k], hg_recv.at[c, k], seq, to
        )

    def dkv_copy(c, k):
        to = lax.rem(seq + k, n_seq)
        return push(
            dkv.at[c, to], rows_of(kv_back, seq, c), dkv_send.at[c, k], dkv_recv.at[c, k], to, grp
        )

    def ring_copy(i, src, dst):
        to = right if i % 2 == 0 else left
        return push(src, dst, ring_send.at[i], ring_recv.at[i], to, grp)

    def core_copy(slot):
        return push(
            cot_ref.at[slot, 0],
            cot_ref.at[slot, 1],
            core_send.at[slot],
            core_recv.at[slot],
            sibling,
            grp,
        )

    def corner(piece):
        return (
            pl.ds(pl.multiple_of((piece % 2) * half, half), half),
            pl.ds(pl.multiple_of((piece // 2) * LANES, LANES), LANES),
        )

    def part_copy(row, piece):
        rows, cols = corner(piece)
        return push(
            term.at[row, rows, cols],
            parts.at[grp],
            part_send.at[row, piece],
            part_recv.at[grp],
            piece,
            2 * seq + row,
        )

    def part_arrival(g):
        return push(
            term.at[0, :half, :LANES],
            parts.at[g],
            part_send.at[0, 0],
            part_recv.at[g],
            source,
            g,
        )

    def each_part(body):
        for row in range(2):

            def step(piece, row=row):
                elsewhere = (piece != seq) | (2 * seq + row != grp)
                pl.when(elsewhere)(lambda: body(row, piece))

            each(n_seq, step)

    def wg_copy(k):
        to = lax.rem(seq + k, n_seq)
        return push(share, wg_out.at[corner(seq)], wg_send.at[k], wg_recv.at[k], to, grp)

    def wg_arrival(k):
        come = lax.rem(seq + n_seq - k, n_seq)
        return push(share, wg_out.at[corner(come)], wg_send.at[k], wg_recv.at[k], come, grp)

    loads[0].wait()
    loads[1].wait()
    for j, cols in enumerate(tiles):
        first, second = weave(k_ref[:, cols], v_ref[:, cols])
        kv_out[2 * j] = first.astype(BF)
        kv_out[2 * j + 1] = second.astype(BF)
    pl.semaphore_wait(barrier, n_seq + n_grp - 2 + 2 * n_seq - jnp.where(keeps_one, 1, 0))
    others(n_seq, lambda k: kv_copy(0, k).start())
    for load in loads[2:]:
        load.wait()
    grad = lax.dot_general(
        c_ref[...], w_ref[...], (((1,), (1,)), ((), ())), preferred_element_type=F32
    ).astype(BF)
    for j, cols in enumerate(tiles):
        first, second = weave(q_ref[:, cols], grad[:, cols])
        qg_out[2 * j] = first.astype(BF)
        qg_out[2 * j + 1] = second.astype(BF)
    cot_ref[0, 0] = c_ref[...]
    qg_in[seq] = qg_out[seq]
    others(n_seq, lambda k: kv_copy(0, k).wait_send())
    others(n_seq, lambda k: kv_copy(1, k).start())

    def pass_on(c):
        mine = kv_in[c]
        mine[seq] = kv_out[seq, c * size : (c + 1) * size]
        others(n_seq, lambda k: kv_copy(c, k).wait_recv())

        def forward(k):
            to = lax.rem(grp + k, n_grp)
            halo_out[c, to] = mine[send_ref[0, 0, to]]
            halo_copy(c, k).start()

        others(n_grp, forward)
        kv_ref[n_seq + grp, c * size : (c + 1) * size] = mine[send_ref[0, 0, grp]]
        kv_ref[:n_seq, c * size : (c + 1) * size] = mine[...]

    pass_on(0)
    others(n_seq, lambda k: kv_copy(1, k).wait_send())
    others(n_seq, lambda k: qg_copy(k).start())
    pass_on(1)

    def turn(i):
        kv_t[i] = kv_ref[i].T

    each(n_seq, turn, 4)
    turn(n_seq + grp)
    others(n_seq, lambda k: qg_copy(k).wait_send())
    rings = [ring_copy(0, cot_ref.at[0, 0], cot_ref.at[1, 0])]
    rings.append(ring_copy(1, cot_ref.at[0, 0], cot_ref.at[2, 0]))
    for copy in rings:
        copy.start()
    core_copy(0).start()
    others(n_seq, lambda k: qg_copy(k).wait_recv())

    def prepare(b):
        x_ref[b] = split_pair(qg_in[b])

    each(n_seq, prepare, 2)

    def take(k):
        for c in range(CHUNKS):
            halo_arrival(c, k).wait_recv()
        turn(n_seq + lax.rem(grp + n_grp - k, n_grp))

    others(n_grp, take)

    for i in range(2, 6):
        rings.append(ring_copy(i, cot_ref.at[i - 1, 0], cot_ref.at[i + 1, 0]))

    def step(i):
        blocks = [i * SIDE + j for j in range(SIDE)]
        attend_blocks(
            blocks, list_ref, count_ref, x_ref, kv_ref, kv_t, aq_out, att_t, terms
        )
        for b in blocks:
            pl.when(b != seq)(aq_copy(b).start)

        @pl.when(i == 0)
        def _():
            for way in range(2):
                rings[way].wait_recv()
                rings[2 + way].start()
                core_copy(1 + way).start()

    each(n_seq // SIDE, step)
    aq_in[seq] = aq_out[seq]

    sums_by_place(plan_ref, 0, terms, running)

    def give(k):
        to = lax.rem(grp + k, n_grp)
        halo_grad[to] = sum_of(n_seq + to, plan_ref, 0, running).astype(BF)
        hg_copy(0, k).start()

    others(n_grp, give)
    mine = sum_of(n_seq + grp, plan_ref, 0, running).astype(BF)
    for c in range(CHUNKS):
        back[c][grp] = mine[c * size : (c + 1) * size]
    for way in range(2):
        rings[2 + way].wait_recv()
        rings[4 + way].start()
        core_copy(3 + way).start()

    def keep(b):
        own_grad[b] = sum_of(b, plan_ref, 0, running)

    each(n_seq, keep, 4)

    def block_of(offset, of_core):
        return lax.rem(seq - core + 2 * offset + n_seq, n_seq) + of_core

    def add(slot):
        core_copy(slot).wait_recv()
        att = jnp.concatenate(
            (att_t[block_of(OFFSETS[slot], core)], att_t[block_of(OFFSETS[slot], 1 - core)]),
            axis=1,
        )
        cot = cot_ref[slot].reshape(att.shape[1], cot_ref.shape[3])
        part = jnp.dot(att, cot, preferred_element_type=F32) * inverse_root
        total[...] = part if slot == 0 else total[...] + part

    for slot in range(3):
        add(slot)
    others(n_grp, lambda k: hg_copy(0, k).wait_send())
    others(n_grp, lambda k: hg_copy(1, k).start())
    for slot in range(3, 5):
        add(slot)
    for way in range(2):
        rings[4 + way].wait_recv()
        where = pl.ds(way * middle, middle)
        rings.append(ring_copy(6 + way, cot_ref.at[5 + way, 0, where], cot_ref.at[7, 0, where]))
        rings[-1].start()
        core_copy(5 + way).start()

    others(n_seq, lambda k: aq_arrival(lax.rem(seq + k, n_seq)).wait_recv())
    for j, cols in enumerate(tiles):
        first, second = weave(aq_in[2 * j], aq_in[2 * j + 1])
        q_ref[:, cols] = first.astype(BF)
        att_n[:, cols] = second.astype(BF)
    k_ref[...] = jnp.dot(att_n[...], w_ref[...], preferred_element_type=F32).astype(BF)
    stores = [local(q_ref, dq_hbm, local_sem.at[0]), local(k_ref, out_hbm, local_sem.at[1])]
    for store in stores:
        store.start()
    for slot in range(5, 7):
        add(slot)

    def settle(c):
        others(n_grp, lambda k: hg_copy(c, k).wait_recv())
        sums_by_place(plan_ref, 4, back[c], back_sum)

        def finish(b):
            more = sum_of(b, plan_ref, 4, back_sum)
            dkv[c, b] = (own_grad[b, c * size : (c + 1) * size] + more).astype(BF)

        each(n_seq, finish, 4)
        others(n_seq, lambda k: dkv_copy(c, k).start())
        stores.append(local(dkv.at[c, seq], rows_of(kv_back, seq, c), local_sem.at[2 + c]))
        stores[-1].start()

    settle(0)
    for way in range(2):
        rings[6 + way].wait_recv()
    core_copy(7).start()
    add(7)
    for row in range(2):
        term[row] = total[2 * half * row : 2 * half * (row + 1)].astype(BF)
    each_part(lambda row, piece: part_copy(row, piece).start())

    @pl.when(keeps_one)
    def _():
        rows, cols = corner(seq)
        parts[grp] = term[lax.rem(grp, 2), rows, cols]

    settle(1)
    each(n_grp, lambda g: from_source(g, part_arrival(g).wait_recv))
    share[...] = jnp.sum(parts[...].astype(F32), axis=0)
    others(n_seq, lambda k: wg_copy(k).start())
    rows, cols = corner(seq)
    wg_out[rows, cols] = share[...]

    for copy in rings:
        copy.wait_send()
    for slot in range(len(OFFSETS)):
        core_copy(slot).wait_send()
    for c in range(CHUNKS):
        others(n_grp, lambda k, c=c: halo_copy(c, k).wait_send())
    others(n_seq, lambda k: aq_copy(lax.rem(seq + k, n_seq)).wait_send())
    others(n_grp, lambda k: hg_copy(1, k).wait_send())
    each_part(lambda row, piece: part_copy(row, piece).wait_send())
    others(n_seq, lambda k: wg_copy(k).wait_send())
    others(n_seq, lambda k: wg_arrival(k).wait_recv())
    for c in range(CHUNKS):
        others(n_seq, lambda k, c=c: dkv_copy(c, k).wait_recv())
        others(n_seq, lambda k, c=c: dkv_copy(c, k).wait_send())
    for store in stores:
        store.wait()


def layer(send, lists, counts, plan, q, k, v, cot, weight, n_seq, n_grp):
    rows, width = q.shape
    tile, part = (rows, LANES), (rows // CHUNKS, LANES)
    per_group = width // n_grp
    space = n_seq + n_grp
    items = lists.shape[1] * lists.shape[2]
    dma = pltpu.SemaphoreType.DMA
    inverse_root = 1.0 / math.sqrt(float(rows * n_seq * n_grp))
    return pl.pallas_call(
        functools.partial(layer_kernel, inverse_root),
        in_specs=[SMEM] * 4 + [ANY] * 5,
        out_specs=(ANY, ANY, ANY, VMEM),
        out_shape=(
            shape(q.shape),
            shape(q.shape),
            shape((n_seq,) + tile),
            shape((per_group, width), F32),
        ),
        scratch_shapes=[pltpu.VMEM(q.shape, BF)] * 4
        + [
            pltpu.VMEM(weight.shape, BF),
            pltpu.VMEM((n_seq,) + tile, BF),
            [pltpu.VMEM((n_seq,) + part, BF)] * CHUNKS,
            pltpu.VMEM((n_seq,) + tile, BF),
            pltpu.VMEM((n_seq,) + tile, BF),
            pltpu.VMEM((CHUNKS, n_grp) + part, BF),
            pltpu.VMEM((space,) + tile, BF),
            pltpu.VMEM((space, LANES, rows), BF),
            pltpu.VMEM((n_seq, 2 * rows, LANES), BF),
            pltpu.VMEM((items,) + tile, F32),
            pltpu.VMEM((items,) + tile, F32),
            pltpu.VMEM((n_seq,) + tile, BF),
            pltpu.VMEM((n_seq,) + tile, BF),
            pltpu.VMEM((n_seq, HD, rows), BF),
            pltpu.VMEM(q.shape, BF),
            pltpu.VMEM((n_seq,) + tile, F32),
            pltpu.VMEM((n_grp,) + tile, BF),
            [pltpu.VMEM((n_grp,) + part, BF)] * CHUNKS,
            pltpu.VMEM((n_grp,) + part, F32),
            pltpu.VMEM((CHUNKS, n_seq) + part, BF),
            pltpu.VMEM((len(OFFSETS), 2) + cot.shape, BF),
            pltpu.VMEM((HD, width), F32),
            pltpu.VMEM((2, per_group, width), BF),
            pltpu.VMEM((n_grp, per_group // 2, LANES), BF),
            pltpu.VMEM((per_group // 2, LANES), F32),
            dma((5,)),
            dma((2 + CHUNKS,)),
            dma((8,)),
            dma((8,)),
            dma((len(OFFSETS),)),
            dma((len(OFFSETS),)),
            dma((CHUNKS, n_seq)),
            dma((CHUNKS, n_seq)),
            dma((n_seq,)),
            dma((n_seq,)),
            dma((CHUNKS, n_grp)),
            dma((CHUNKS, n_grp)),
            dma((n_seq,)),
            dma((n_seq,)),
            dma((CHUNKS, n_grp)),
            dma((CHUNKS, n_grp)),
            dma((CHUNKS, n_seq)),
            dma((CHUNKS, n_seq)),
            dma((2, n_seq)),
            dma((n_grp,)),
            dma((n_seq,)),
            dma((n_seq,)),
        ],
        compiler_params=pltpu.CompilerParams(
            vmem_limit_bytes=LIMIT, collective_id=0, has_side_effects=True
        ),
    )(send, lists, counts, plan, q, k, v, cot, weight)


def finish_kernel(out_in, dq_in, kv_ref, wg_in, out_ref, dq_ref, dk_ref, dv_ref, wg_ref):
    out_ref[...] = out_in[...]
    dq_ref[...] = dq_in[...]
    wg_ref[...] = wg_in[...]
    for j in range(kv_ref.shape[0] // 2):
        cols = slice(j * LANES, (j + 1) * LANES)
        first, second = weave(kv_ref[2 * j], kv_ref[2 * j + 1])
        dk_ref[:, cols] = first.astype(BF)
        dv_ref[:, cols] = second.astype(BF)


def per_device(
    queries, key_rows, value_rows, cotangent, out_weight, send_lists, key_blocks, key_counts
):
    send = send_lists.transpose(0, 2, 1)
    lists = key_blocks.transpose(0, 2, 1)
    out, dq, dkv, weight_grad = layer(
        send,
        lists,
        key_counts,
        make_plan(send, lists),
        queries,
        key_rows,
        value_rows,
        cotangent,
        out_weight,
        lax.axis_size("seq"),
        lax.axis_size("grp"),
    )
    flat = shape(queries.shape)
    return pl.pallas_call(
        finish_kernel,
        in_specs=[VMEM] * 4,
        out_specs=(VMEM,) * 5,
        out_shape=(flat,) * 4 + (shape(weight_grad.shape, F32),),
        compiler_params=pltpu.CompilerParams(vmem_limit_bytes=LIMIT),
    )(out, dq, dkv, weight_grad)


def solution(mesh):
    nodes = P(("seq", "grp"), None)
    by_group = P("grp", None, None)
    return jax.shard_map(
        per_device,
        mesh=mesh,
        in_specs=(nodes, nodes, nodes, nodes, P(), by_group, by_group, P("grp", None)),
        out_specs=(nodes, nodes, nodes, nodes, P("grp", None)),
        check_vma=False,
    )
```

time: 401 us -> 118 us (0.29)
  waiting for transfers between devices: 210 us -> 0 us
  blocking collectives: 110 us -> 0 us
  Pallas kernels: 22.7 us -> 115 us
  starting transfers between devices: 26 us -> 0 us
  between operations: 14.9 us -> 0.64 us
  local copies, waits for them, and re-layouts: 13.8 us -> 0 us
    unnamed x3 -> x0, waiting for transfers between devices: 144 us -> none
    pallas_call x4 -> x3, Pallas kernels: 22.7 us -> 115 us  [the longest x1 111 us: layer(): pl.pallas_call(functools.partial(layer_kernel, inverse_root), in_specs=[S...]
    all_to_all x3 -> x0, blocking collectives: 88 us -> none  [the longest x1 41.4 us: per_device(): lax.all_to_all(kv[send_lists[0, :, 0]], 'grp', split_axis=0, concat_axis=...]
    all_to_all x4 -> x0, waiting for transfers between devices: 66.2 us -> none  [the longest x1 20 us: per_device(): kv = lax.all_to_all(kv, 'seq', split_axis=0, concat_axis=0, tiled=True)]
    all_to_all x4 -> x0, starting transfers between devices: 25.9 us -> none  [the longest x1 10.2 us: per_device(): kv = lax.all_to_all(kv, 'seq', split_axis=0, concat_axis=0, tiled=True)]
    all_gather x1 -> x0, blocking collectives: 22.2 us -> none  [per_device(): part = lax.all_gather(part, 'seq', axis=0, tiled=False)]
    unnamed x30 -> x0, local copies, waits for them, and re-layouts: 11.4 us -> none
  transfers between devices with their start and end apart: 6 -> 0, of which waited for: 5 -> 0; matrix products, arithmetic and copies ran while one was open for 1% -> 0% of each run, Pallas kernels for 1% -> 0%
where the time goes in v3:
time: 118 us; the launch traced here: 116 us
  Pallas kernels  115 us (97%)
    pallas_call x1, Pallas kernels, layer(): pl.pallas_call(functools.partial(layer_kernel, inverse_root), in_specs=[S...  111 us
    pallas_call x1, Pallas kernels, per_device(): pl.pallas_call(finish_kernel, in_specs=[VMEM] * 4, out_specs=(VMEM,) * 5,...  2.42 us

profile of v3, /device:TPU:1, one launch (start us, length us, event | category | flops | bytes accessed | tf_op | source)
XLA Modules:
  0.0 116.1 jit_solution(12643584859655472257)
XLA Ops:
  0.6 2.2 %shard_map.119.plan_ref = s32[8,128]{1,0:T(8,128)} custom-call(s32[1,1,32]{2,1,0:T(1,128)} %bitcast.4, s32[1,8,16]{2,1,0:T(8,128)} %bitcast.2), custom_call_target="tpu_custom_call" | custom-call | tf_op jit(solution)/shard_map/pallas_call | solution.py:115
  2.8 110.8 %shard_map.120 = (bf16[128,1024]{1,0:T(8,128)(2,1)}, bf16[128,1024]{1,0:T(8,128)(2,1)}, bf16[16,128,128]{2,1,0:T(8,128)(2,1)}, f32[32,1024]{1,0:T(8,128)}) custom-call(s32[1,1,32]{2,1,0:T(1,128)} %bitcast.5, s32[1,8,16]{2,1,0:T(8,128)} %bitcast.3, s32[1,16]{1,0:T(1,128)} %count_ref.1, s32[8,128]{1,0:T(8,128)} %shard_map.119.plan_ref, ...), custom_call_target="tpu_custom_call" | custom-call | tf_op jit(solution)/shard_map/pallas_call | solution.py:605
  113.6 2.4 %shard_map.121 = (bf16[128,1024]{1,0:T(8,128)(2,1)}, bf16[128,1024]{1,0:T(8,128)(2,1)}, bf16[128,1024]{1,0:T(8,128)(2,1)}, bf16[128,1024]{1,0:T(8,128)(2,1)}, f32[32,1024]{1,0:T(8,128)}) custom-call(bf16[128,1024]{1,0:T(8,128)(2,1)} %get-tuple-element.9.out_in, bf16[128,1024]{1,0:T(8,128)(2,1)} %get-tuple-element.10.dq_in, ...), custom_call_target="tpu_custom_call" | custom-call | tf_op jit(solution)/shard_map/pallas_call | solution.py:701

commit v4 on v3

--- a/solution.py
+++ b/solution.py
@@ -16,7 +16,8 @@
 SMEM = pl.BlockSpec(memory_space=pltpu.SMEM)
 ANY = pl.BlockSpec(memory_space=pl.ANY)
 LIMIT = 60 * 1024 * 1024
-CHUNKS = 2
+THERE = (64, 64)
+BACK = (64, 64)
 MESH = pl.DeviceIdType.MESH
 
 
@@ -67,9 +68,12 @@
     return pltpu.make_async_copy(src, dst, semaphore)
 
 
-def rows_of(ref, block, chunk):
-    rows = ref.shape[1] // CHUNKS
-    return ref.at[block, pl.ds(chunk * rows, rows)]
+def span_of(sizes, c):
+    return slice(sum(sizes[:c]), sum(sizes[: c + 1]))
+
+
+def rows_of(ref, block, sizes, c):
+    return ref.at[block, pl.ds(sum(sizes[:c]), sizes[c])]
 
 
 def place_order(place):
@@ -240,6 +244,7 @@
     term,
     parts,
     share,
+    wg_in,
     load_sem,
     local_sem,
     ring_send,
@@ -265,12 +270,12 @@
 ):
     seq, grp = lax.axis_index("seq"), lax.axis_index("grp")
     n_seq, n_grp = qg_in.shape[0], halo_grad.shape[0]
-    size = kv_in[0].shape[1]
     half = wg_out.shape[0] // 2
     middle = cot_ref.shape[2] // 2
     right, left = lax.rem(seq + 2, n_seq), lax.rem(seq + n_seq - 2, n_seq)
     core = lax.rem(seq, 2)
     sibling = seq + 1 - 2 * core
+    next_grp = lax.rem(grp + 1, n_grp)
     source = grp // 2
     keeps_one = source == seq
     tiles = [slice(j * LANES, (j + 1) * LANES) for j in range(n_seq // 2)]
@@ -283,60 +288,68 @@
     others(n_seq, lambda k: signal(barrier, lax.rem(seq + k, n_seq), grp))
     others(n_grp, lambda k: signal(barrier, seq, lax.rem(grp + k, n_grp)))
 
-    def from_source(g, body):
-        pl.when((source != seq) | (g != grp))(body)
-
-    each(n_grp, lambda g: from_source(g, lambda: signal(barrier, source, g)))
-
-    def kv_copy(c, k):
-        to = lax.rem(seq + k, n_seq)
-        return push(
-            rows_of(kv_out, to, c), kv_in[c].at[seq], kv_send.at[c, k], kv_recv.at[c, k], to, grp
-        )
-
-    def qg_copy(k):
-        to = lax.rem(seq + k, n_seq)
-        return push(qg_out.at[to], qg_in.at[seq], qg_send.at[k], qg_recv.at[k], to, grp)
-
-    def halo_copy(c, k):
-        to = lax.rem(grp + k, n_grp)
-        return push(
-            halo_out.at[c, to],
-            rows_of(kv_ref, n_seq + grp, c),
-            halo_send.at[c, k],
-            halo_recv.at[c, k],
-            seq,
-            to,
-        )
-
-    def halo_arrival(c, k):
-        come = lax.rem(grp + n_grp - k, n_grp)
-        return push(
-            halo_out.at[c, come],
-            rows_of(kv_ref, n_seq + come, c),
-            halo_send.at[c, k],
-            halo_recv.at[c, k],
-            seq,
-            come,
-        )
-
-    def aq_copy(b):
-        return push(aq_out.at[b], aq_in.at[seq], aq_send.at[b], aq_recv.at[seq], b, grp)
-
-    def aq_arrival(b):
-        return push(aq_out.at[b], aq_in.at[b], aq_send.at[b], aq_recv.at[b], b, grp)
-
-    def hg_copy(c, k):
-        to = lax.rem(grp + k, n_grp)
-        return push(
-            rows_of(halo_grad, to, c), back[c].at[grp], hg_send.at[c, k], hg_recv.at[c, k], seq, to
-        )
-
-    def dkv_copy(c, k):
-        to = lax.rem(seq + k, n_seq)
-        return push(
-            dkv.at[c, to], rows_of(kv_back, seq, c), dkv_send.at[c, k], dkv_recv.at[c, k], to, grp
-        )
+    def greet(g):
+        pl.when((source != seq) | (g != grp))(lambda: signal(barrier, source, g))
+
+    each(n_grp, greet)
+
+    most, rest = pl.ds(0, n_seq - 1), pl.ds(0, n_grp - 1)
+
+    def kv_copy(c, to, src=None, dst=None):
+        src = rows_of(kv_out, to, THERE, c) if src is None else src
+        dst = kv_in[c].at[seq] if dst is None else dst
+        return push(src, dst, kv_send.at[c], kv_recv.at[c], to, grp)
+
+    def all_kv(c):
+        src = rows_of(kv_out, most, THERE, c)
+        return kv_copy(c, sibling, src, kv_in[c].at[most])
+
+    def qg_copy(to, src=None, dst=None):
+        src = qg_out.at[to] if src is None else src
+        dst = qg_in.at[seq] if dst is None else dst
+        return push(src, dst, qg_send, qg_recv, to, grp)
+
+    def all_qg():
+        return qg_copy(sibling, qg_out.at[most], qg_in.at[most])
+
+    def halo_copy(c, to, src=None, dst=None):
+        src = halo_out[c].at[to] if src is None else src
+        dst = rows_of(kv_ref, n_seq + grp, THERE, c) if dst is None else dst
+        return push(src, dst, halo_send.at[c], halo_recv.at[c], seq, to)
+
+    def all_halo(c):
+        dst = rows_of(kv_ref, pl.ds(n_seq, n_grp - 1), THERE, c)
+        return halo_copy(c, next_grp, halo_out[c].at[rest], dst)
+
+    def aq_copy(to, src=None, dst=None):
+        src = aq_out.at[to] if src is None else src
+        dst = aq_in.at[seq] if dst is None else dst
+        return push(src, dst, aq_send, aq_recv, to, grp)
+
+    def all_aq():
+        return aq_copy(sibling, aq_out.at[most], aq_in.at[most])
+
+    def hg_copy(c, to, src=None, dst=None):
+        src = rows_of(halo_grad, to, BACK, c) if src is None else src
+        dst = back[c].at[grp] if dst is None else dst
+        return push(src, dst, hg_send.at[c], hg_recv.at[c], seq, to)
+
+    def all_hg(c):
+        return hg_copy(c, next_grp, rows_of(halo_grad, rest, BACK, c), back[c].at[rest])
+
+    def dkv_copy(c, to, src=None, dst=None):
+        src = dkv[c].at[to] if src is None else src
+        dst = rows_of(kv_back, seq, BACK, c) if dst is None else dst
+        return push(src, dst, dkv_send.at[c], dkv_recv.at[c], to, grp)
+
+    def all_dkv(c):
+        return dkv_copy(c, sibling, dkv[c].at[most], rows_of(kv_back, most, BACK, c))
+
+    def to_seq(body):
+        others(n_seq, lambda k: body(lax.rem(seq + k, n_seq)))
+
+    def to_grp(body):
+        others(n_grp, lambda k: body(lax.rem(grp + k, n_grp)))
 
     def ring_copy(i, src, dst):
         to = right if i % 2 == 0 else left
@@ -361,23 +374,14 @@
     def part_copy(row, piece):
         rows, cols = corner(piece)
         return push(
-            term.at[row, rows, cols],
-            parts.at[grp],
-            part_send.at[row, piece],
-            part_recv.at[grp],
-            piece,
-            2 * seq + row,
+            term.at[row, rows, cols], parts.at[grp], part_send, part_recv, piece, 2 * seq + row
         )
 
-    def part_arrival(g):
-        return push(
-            term.at[0, :half, :LANES],
-            parts.at[g],
-            part_send.at[0, 0],
-            part_recv.at[g],
-            source,
-            g,
-        )
+    def all_parts(body):
+        for mine in (0, 1):
+            every = parts.at[pl.ds(0, n_grp - mine)]
+            copy = push(every, every, part_send, part_recv, sibling, grp)
+            pl.when(keeps_one if mine else jnp.logical_not(keeps_one))(functools.partial(body, copy))
 
     def each_part(body):
         for row in range(2):
@@ -388,13 +392,11 @@
 
             each(n_seq, step)
 
-    def wg_copy(k):
-        to = lax.rem(seq + k, n_seq)
-        return push(share, wg_out.at[corner(seq)], wg_send.at[k], wg_recv.at[k], to, grp)
-
-    def wg_arrival(k):
-        come = lax.rem(seq + n_seq - k, n_seq)
-        return push(share, wg_out.at[corner(come)], wg_send.at[k], wg_recv.at[k], come, grp)
+    def wg_copy(to):
+        return push(share, wg_in.at[seq], wg_send, wg_recv, to, grp)
+
+    def all_wg():
+        return push(wg_in.at[most], wg_in.at[most], wg_send, wg_recv, sibling, grp)
 
     loads[0].wait()
     loads[1].wait()
@@ -403,7 +405,7 @@
         kv_out[2 * j] = first.astype(BF)
         kv_out[2 * j + 1] = second.astype(BF)
     pl.semaphore_wait(barrier, n_seq + n_grp - 2 + 2 * n_seq - jnp.where(keeps_one, 1, 0))
-    others(n_seq, lambda k: kv_copy(0, k).start())
+    to_seq(lambda to: kv_copy(0, to).start())
     for load in loads[2:]:
         load.wait()
     grad = lax.dot_general(
@@ -415,55 +417,54 @@
         qg_out[2 * j + 1] = second.astype(BF)
     cot_ref[0, 0] = c_ref[...]
     qg_in[seq] = qg_out[seq]
-    others(n_seq, lambda k: kv_copy(0, k).wait_send())
-    others(n_seq, lambda k: kv_copy(1, k).start())
-
     def pass_on(c):
-        mine = kv_in[c]
-        mine[seq] = kv_out[seq, c * size : (c + 1) * size]
-        others(n_seq, lambda k: kv_copy(c, k).wait_recv())
-
-        def forward(k):
-            to = lax.rem(grp + k, n_grp)
-            halo_out[c, to] = mine[send_ref[0, 0, to]]
-            halo_copy(c, k).start()
-
-        others(n_grp, forward)
-        kv_ref[n_seq + grp, c * size : (c + 1) * size] = mine[send_ref[0, 0, grp]]
-        kv_ref[:n_seq, c * size : (c + 1) * size] = mine[...]
-
-    pass_on(0)
-    others(n_seq, lambda k: kv_copy(1, k).wait_send())
-    others(n_seq, lambda k: qg_copy(k).start())
-    pass_on(1)
+        mine, span = kv_in[c], span_of(THERE, c)
+        mine[seq] = kv_out[seq, span]
+        all_kv(c).wait_recv()
+
+        def forward(to):
+            halo_out[c][to] = mine[send_ref[0, 0, to]]
+            halo_copy(c, to).start()
+
+        to_grp(forward)
+        kv_ref[n_seq + grp, span] = mine[send_ref[0, 0, grp]]
+        kv_ref[:n_seq, span] = mine[...]
+
+    for c in range(1, len(THERE)):
+        all_kv(c - 1).wait_send()
+        to_seq(lambda to, c=c: kv_copy(c, to).start())
+        pass_on(c - 1)
+    all_kv(len(THERE) - 1).wait_send()
+    to_seq(lambda to: qg_copy(to).start())
+    pass_on(len(THERE) - 1)
 
     def turn(i):
         kv_t[i] = kv_ref[i].T
 
     each(n_seq, turn, 4)
-    turn(n_seq + grp)
-    others(n_seq, lambda k: qg_copy(k).wait_send())
+    all_qg().wait_send()
     rings = [ring_copy(0, cot_ref.at[0, 0], cot_ref.at[1, 0])]
     rings.append(ring_copy(1, cot_ref.at[0, 0], cot_ref.at[2, 0]))
     for copy in rings:
         copy.start()
     core_copy(0).start()
-    others(n_seq, lambda k: qg_copy(k).wait_recv())
+    all_qg().wait_recv()
 
     def prepare(b):
         x_ref[b] = split_pair(qg_in[b])
 
     each(n_seq, prepare, 2)
-
-    def take(k):
-        for c in range(CHUNKS):
-            halo_arrival(c, k).wait_recv()
-        turn(n_seq + lax.rem(grp + n_grp - k, n_grp))
-
-    others(n_grp, take)
-
+    for c in range(len(THERE)):
+        all_halo(c).wait_recv()
+    each(n_grp, lambda g: turn(n_seq + g), 4)
     for i in range(2, 6):
         rings.append(ring_copy(i, cot_ref.at[i - 1, 0], cot_ref.at[i + 1, 0]))
+
+    def ring_step(first):
+        for way in range(2):
+            rings[first + way].wait_recv()
+            rings[first + 2 + way].start()
+            core_copy(first + 1 + way).start()
 
     def step(i):
         blocks = [i * SIDE + j for j in range(SIDE)]
@@ -472,32 +473,22 @@
         )
         for b in blocks:
             pl.when(b != seq)(aq_copy(b).start)
-
-        @pl.when(i == 0)
-        def _():
-            for way in range(2):
-                rings[way].wait_recv()
-                rings[2 + way].start()
-                core_copy(1 + way).start()
+        pl.when(i == 0)(lambda: ring_step(0))
 
     each(n_seq // SIDE, step)
     aq_in[seq] = aq_out[seq]
 
     sums_by_place(plan_ref, 0, terms, running)
 
-    def give(k):
-        to = lax.rem(grp + k, n_grp)
+    def give(to):
         halo_grad[to] = sum_of(n_seq + to, plan_ref, 0, running).astype(BF)
-        hg_copy(0, k).start()
-
-    others(n_grp, give)
+        hg_copy(0, to).start()
+
+    to_grp(give)
     mine = sum_of(n_seq + grp, plan_ref, 0, running).astype(BF)
-    for c in range(CHUNKS):
-        back[c][grp] = mine[c * size : (c + 1) * size]
-    for way in range(2):
-        rings[2 + way].wait_recv()
-        rings[4 + way].start()
-        core_copy(3 + way).start()
+    for c in range(len(BACK)):
+        back[c][grp] = mine[span_of(BACK, c)]
+    ring_step(2)
 
     def keep(b):
         own_grad[b] = sum_of(b, plan_ref, 0, running)
@@ -517,12 +508,11 @@
         part = jnp.dot(att, cot, preferred_element_type=F32) * inverse_root
         total[...] = part if slot == 0 else total[...] + part
 
-    for slot in range(3):
+    for slot in range(5):
         add(slot)
-    others(n_grp, lambda k: hg_copy(0, k).wait_send())
-    others(n_grp, lambda k: hg_copy(1, k).start())
-    for slot in range(3, 5):
-        add(slot)
+    for c in range(1, len(BACK)):
+        all_hg(c - 1).wait_send()
+        to_grp(lambda to, c=c: hg_copy(c, to).start())
     for way in range(2):
         rings[4 + way].wait_recv()
         where = pl.ds(way * middle, middle)
@@ -530,7 +520,7 @@
         rings[-1].start()
         core_copy(5 + way).start()
 
-    others(n_seq, lambda k: aq_arrival(lax.rem(seq + k, n_seq)).wait_recv())
+    all_aq().wait_recv()
     for j, cols in enumerate(tiles):
         first, second = weave(aq_in[2 * j], aq_in[2 * j + 1])
         q_ref[:, cols] = first.astype(BF)
@@ -543,19 +533,21 @@
         add(slot)
 
     def settle(c):
-        others(n_grp, lambda k: hg_copy(c, k).wait_recv())
-        sums_by_place(plan_ref, 4, back[c], back_sum)
+        span = span_of(BACK, c)
+        all_hg(c).wait_recv()
+        sums_by_place(plan_ref, 4, back[c], back_sum[c])
 
         def finish(b):
-            more = sum_of(b, plan_ref, 4, back_sum)
-            dkv[c, b] = (own_grad[b, c * size : (c + 1) * size] + more).astype(BF)
+            more = sum_of(b, plan_ref, 4, back_sum[c])
+            dkv[c][b] = (own_grad[b, span] + more).astype(BF)
 
         each(n_seq, finish, 4)
-        others(n_seq, lambda k: dkv_copy(c, k).start())
-        stores.append(local(dkv.at[c, seq], rows_of(kv_back, seq, c), local_sem.at[2 + c]))
+        to_seq(lambda to: dkv_copy(c, to).start())
+        stores.append(local(dkv[c].at[seq], rows_of(kv_back, seq, BACK, c), local_sem.at[2 + c]))
         stores[-1].start()
 
-    settle(0)
+    for c in range(len(BACK) - 1):
+        settle(c)
     for way in range(2):
         rings[6 + way].wait_recv()
     core_copy(7).start()
@@ -569,34 +561,37 @@
         rows, cols = corner(seq)
         parts[grp] = term[lax.rem(grp, 2), rows, cols]
 
-    settle(1)
-    each(n_grp, lambda g: from_source(g, part_arrival(g).wait_recv))
+    settle(len(BACK) - 1)
+    all_parts(lambda copy: copy.wait_recv())
     share[...] = jnp.sum(parts[...].astype(F32), axis=0)
-    others(n_seq, lambda k: wg_copy(k).start())
-    rows, cols = corner(seq)
-    wg_out[rows, cols] = share[...]
+    to_seq(lambda to: wg_copy(to).start())
+    wg_in[seq] = share[...]
 
     for copy in rings:
         copy.wait_send()
     for slot in range(len(OFFSETS)):
         core_copy(slot).wait_send()
-    for c in range(CHUNKS):
-        others(n_grp, lambda k, c=c: halo_copy(c, k).wait_send())
-    others(n_seq, lambda k: aq_copy(lax.rem(seq + k, n_seq)).wait_send())
-    others(n_grp, lambda k: hg_copy(1, k).wait_send())
-    each_part(lambda row, piece: part_copy(row, piece).wait_send())
-    others(n_seq, lambda k: wg_copy(k).wait_send())
-    others(n_seq, lambda k: wg_arrival(k).wait_recv())
-    for c in range(CHUNKS):
-        others(n_seq, lambda k, c=c: dkv_copy(c, k).wait_recv())
-        others(n_seq, lambda k, c=c: dkv_copy(c, k).wait_send())
+    for c in range(len(THERE)):
+        all_halo(c).wait_send()
+    all_aq().wait_send()
+    all_hg(len(BACK) - 1).wait_send()
+    all_parts(lambda copy: copy.wait_send())
+    all_wg().wait_send()
+    all_wg().wait_recv()
+    for piece in range(n_seq):
+        rows, cols = corner(piece)
+        wg_out[rows, cols] = wg_in[piece]
+    for c in range(len(BACK)):
+        all_dkv(c).wait_send()
+    for c in range(len(BACK)):
+        all_dkv(c).wait_recv()
     for store in stores:
         store.wait()
 
 
 def layer(send, lists, counts, plan, q, k, v, cot, weight, n_seq, n_grp):
     rows, width = q.shape
-    tile, part = (rows, LANES), (rows // CHUNKS, LANES)
+    tile = (rows, LANES)
     per_group = width // n_grp
     space = n_seq + n_grp
     items = lists.shape[1] * lists.shape[2]
@@ -616,10 +611,10 @@
         + [
             pltpu.VMEM(weight.shape, BF),
             pltpu.VMEM((n_seq,) + tile, BF),
-            [pltpu.VMEM((n_seq,) + part, BF)] * CHUNKS,
+            [pltpu.VMEM((n_seq, size, LANES), BF) for size in THERE],
             pltpu.VMEM((n_seq,) + tile, BF),
             pltpu.VMEM((n_seq,) + tile, BF),
-            pltpu.VMEM((CHUNKS, n_grp) + part, BF),
+            [pltpu.VMEM((n_grp, size, LANES), BF) for size in THERE],
             pltpu.VMEM((space,) + tile, BF),
             pltpu.VMEM((space, LANES, rows), BF),
             pltpu.VMEM((n_seq, 2 * rows, LANES), BF),
@@ -631,36 +626,37 @@
             pltpu.VMEM(q.shape, BF),
             pltpu.VMEM((n_seq,) + tile, F32),
             pltpu.VMEM((n_grp,) + tile, BF),
-            [pltpu.VMEM((n_grp,) + part, BF)] * CHUNKS,
-            pltpu.VMEM((n_grp,) + part, F32),
-            pltpu.VMEM((CHUNKS, n_seq) + part, BF),
+            [pltpu.VMEM((n_grp, size, LANES), BF) for size in BACK],
+            [pltpu.VMEM((n_grp, size, LANES), F32) for size in BACK],
+            [pltpu.VMEM((n_seq, size, LANES), BF) for size in BACK],
             pltpu.VMEM((len(OFFSETS), 2) + cot.shape, BF),
             pltpu.VMEM((HD, width), F32),
             pltpu.VMEM((2, per_group, width), BF),
             pltpu.VMEM((n_grp, per_group // 2, LANES), BF),
             pltpu.VMEM((per_group // 2, LANES), F32),
+            pltpu.VMEM((n_seq, per_group // 2, LANES), F32),
             dma((5,)),
-            dma((2 + CHUNKS,)),
+            dma((2 + len(BACK),)),
             dma((8,)),
             dma((8,)),
             dma((len(OFFSETS),)),
             dma((len(OFFSETS),)),
-            dma((CHUNKS, n_seq)),
-            dma((CHUNKS, n_seq)),
-            dma((n_seq,)),
-            dma((n_seq,)),
-            dma((CHUNKS, n_grp)),
-            dma((CHUNKS, n_grp)),
-            dma((n_seq,)),
-            dma((n_seq,)),
-            dma((CHUNKS, n_grp)),
-            dma((CHUNKS, n_grp)),
-            dma((CHUNKS, n_seq)),
-            dma((CHUNKS, n_seq)),
-            dma((2, n_seq)),
-            dma((n_grp,)),
-            dma((n_seq,)),
-            dma((n_seq,)),
+            dma((len(THERE),)),
+            dma((len(THERE),)),
+            dma,
+            dma,
+            dma((len(THERE),)),
+            dma((len(THERE),)),
+            dma,
+            dma,
+            dma((len(BACK),)),
+            dma((len(BACK),)),
+            dma((len(BACK),)),
+            dma((len(BACK),)),
+            dma,
+            dma,
+            dma,
+            dma,
         ],
         compiler_params=pltpu.CompilerParams(
             vmem_limit_bytes=LIMIT, collective_id=0, has_side_effects=True

time: 118 us -> 112 us (0.949)
  Pallas kernels: 115 us -> 110 us
    pallas_call x1, Pallas kernels: 111 us -> 105 us  [layer(): pl.pallas_call(functools.partial(layer_kernel, inverse_root), in_specs=[S...]
where the time goes in v4:
time: 112 us; the launch traced here: 110 us
  Pallas kernels  110 us (98%)
    pallas_call x1, Pallas kernels, layer(): pl.pallas_call(functools.partial(layer_kernel, inverse_root), in_specs=[S...  105 us
    pallas_call x1, Pallas kernels, per_device(): pl.pallas_call(finish_kernel, in_specs=[VMEM] * 4, out_specs=(VMEM,) * 5,...  2.42 us

profile of v4, /device:TPU:1, one launch (start us, length us, event | category | flops | bytes accessed | tf_op | source)
XLA Modules:
  0.0 110.3 jit_solution(10820788147726924777)
XLA Ops:
  0.6 2.2 %shard_map.119.plan_ref = s32[8,128]{1,0:T(8,128)} custom-call(s32[1,1,32]{2,1,0:T(1,128)} %bitcast.4, s32[1,8,16]{2,1,0:T(8,128)} %bitcast.2), custom_call_target="tpu_custom_call" | custom-call | tf_op jit(solution)/shard_map/pallas_call | solution.py:119
  2.8 105.0 %shard_map.120 = (bf16[128,1024]{1,0:T(8,128)(2,1)}, bf16[128,1024]{1,0:T(8,128)(2,1)}, bf16[16,128,128]{2,1,0:T(8,128)(2,1)}, f32[32,1024]{1,0:T(8,128)}) custom-call(s32[1,1,32]{2,1,0:T(1,128)} %bitcast.5, s32[1,8,16]{2,1,0:T(8,128)} %bitcast.3, s32[1,16]{1,0:T(1,128)} %count_ref.1, s32[8,128]{1,0:T(8,128)} %shard_map.119.plan_ref, ...), custom_call_target="tpu_custom_call" | custom-call | tf_op jit(solution)/shard_map/pallas_call | solution.py:600
  107.9 2.4 %shard_map.121 = (bf16[128,1024]{1,0:T(8,128)(2,1)}, bf16[128,1024]{1,0:T(8,128)(2,1)}, bf16[128,1024]{1,0:T(8,128)(2,1)}, bf16[128,1024]{1,0:T(8,128)(2,1)}, f32[32,1024]{1,0:T(8,128)}) custom-call(bf16[128,1024]{1,0:T(8,128)(2,1)} %get-tuple-element.9.out_in, bf16[128,1024]{1,0:T(8,128)(2,1)} %get-tuple-element.10.dq_in, ...), custom_call_target="tpu_custom_call" | custom-call | tf_op jit(solution)/shard_map/pallas_call | solution.py:697

commit v5 on v4

--- a/solution.py
+++ b/solution.py
@@ -77,26 +77,24 @@
 
 
 def place_order(place):
-    row = lax.broadcasted_iota(jnp.int32, place.shape, 0).astype(F32)
-    col = lax.broadcasted_iota(jnp.int32, place.shape, 1).astype(F32)
+    row = lax.broadcasted_iota(jnp.int32, place.shape, 0)
+    col = lax.broadcasted_iota(jnp.int32, place.shape, 1)
     other = place.T
     earlier = (other < place) | ((other == place) & (col < row))
-    rank = jnp.sum(jnp.where(earlier, 1.0, 0.0), axis=1, keepdims=True)
+    rank = jnp.sum(jnp.where(earlier, 1, 0), axis=1, keepdims=True)
     there = rank == col
 
     def down(mask, value):
-        return jnp.sum(jnp.where(mask, value, 0.0), axis=0, keepdims=True)
+        return jnp.sum(jnp.where(mask, value, 0), axis=0, keepdims=True)
 
     order = down(there, row)
     sorted_place = down(there, place)
-    again = (sorted_place == pltpu.roll(sorted_place, 1, 1)) & (col[:1] > 0.0)
-    last = jnp.maximum(down(place <= col, 1.0) - 1.0, 0.0)
-    return jnp.concatenate(
-        (order, jnp.where(again, 1.0, 0.0), last, down(place == col, 1.0)), axis=0
-    ).astype(jnp.int32)
-
-
-def plan_kernel(send_ref, list_ref, plan_ref, place):
+    again = (sorted_place == pltpu.roll(sorted_place, 1, 1)) & (col[:1] > 0)
+    last = jnp.maximum(down(place <= col, 1) - 1, 0)
+    return jnp.concatenate((order, jnp.where(again, 1, 0), last, down(place == col, 1)), axis=0)
+
+
+def make_plan(send_ref, list_ref, place, plan):
     listed, blocks = list_ref.shape[1:]
     groups = send_ref.shape[2]
 
@@ -108,21 +106,10 @@
             put(b * listed + t, list_ref[0, t, b])
 
     each(blocks, pairs)
-    for_pairs = place_order(place[...].astype(F32))
+    for_pairs = place_order(place[...])
     place[...] = jnp.full(place.shape, place.shape[1], jnp.int32)
     each(groups, lambda g: put(g, send_ref[0, 0, g]))
-    plan_ref[...] = jnp.concatenate((for_pairs, place_order(place[...].astype(F32))), axis=0)
-
-
-def make_plan(send, lists):
-    items = lists.shape[1] * lists.shape[2]
-    return pl.pallas_call(
-        plan_kernel,
-        in_specs=[SMEM] * 2,
-        out_specs=VMEM,
-        out_shape=shape((8, items), jnp.int32),
-        scratch_shapes=[pltpu.VMEM((items, items), jnp.int32)],
-    )(send, lists)
+    plan[...] = jnp.concatenate((for_pairs, place_order(place[...])), axis=0)
 
 
 def split_pair(pair):
@@ -182,18 +169,20 @@
         aq_ref[b] = jnp.concatenate((out[:HD, :rows] * scale, attended), axis=0).T.astype(BF)
 
 
-def sums_by_place(plan_ref, at, source, running):
+def sums_by_place(plan_ref, at, source, running, span=slice(None)):
     def run(j, total):
         total = jnp.where(plan_ref[at + 1, j] != 0, total, 0.0)
-        total = total + source[plan_ref[at, j]].astype(F32)
-        running[j] = total
+        total = total + source[plan_ref[at, j], span].astype(F32)
+        running[j, span] = total
         return total
 
-    lax.fori_loop(0, running.shape[0], run, jnp.zeros(running.shape[1:], F32), unroll=4)
-
-
-def sum_of(place, plan_ref, at, running):
-    return jnp.where(plan_ref[at + 3, place] != 0, running[plan_ref[at + 2, place]], 0.0)
+    rows = len(range(*span.indices(running.shape[1])))
+    zero = jnp.zeros((rows, running.shape[2]), F32)
+    lax.fori_loop(0, running.shape[0], run, zero, unroll=4)
+
+
+def sum_of(place, plan_ref, at, running, span=slice(None)):
+    return jnp.where(plan_ref[at + 3, place] != 0, running[plan_ref[at + 2, place], span], 0.0)
 
 
 OFFSETS = (0, -1, 1, -2, 2, -3, 3, 4)
@@ -205,7 +194,6 @@
     send_ref,
     list_ref,
     count_ref,
-    plan_ref,
     q_hbm,
     k_hbm,
     v_hbm,
@@ -245,6 +233,9 @@
     parts,
     share,
     wg_in,
+    place,
+    plan,
+    plan_ref,
     load_sem,
     local_sem,
     ring_send,
@@ -438,10 +429,13 @@
     to_seq(lambda to: qg_copy(to).start())
     pass_on(len(THERE) - 1)
 
-    def turn(i):
-        kv_t[i] = kv_ref[i].T
+    def turn(i, span=slice(None)):
+        kv_t[i, :, span] = kv_ref[i, span].T
 
     each(n_seq, turn, 4)
+    make_plan(send_ref, list_ref, place, plan)
+    plan_load = local(plan, plan_ref, load_sem.at[5])
+    plan_load.start()
     all_qg().wait_send()
     rings = [ring_copy(0, cot_ref.at[0, 0], cot_ref.at[1, 0])]
     rings.append(ring_copy(1, cot_ref.at[0, 0], cot_ref.at[2, 0]))
@@ -456,7 +450,7 @@
     each(n_seq, prepare, 2)
     for c in range(len(THERE)):
         all_halo(c).wait_recv()
-    each(n_grp, lambda g: turn(n_seq + g), 4)
+        each(n_grp, lambda g, c=c: turn(n_seq + g, span_of(THERE, c)), 4)
     for i in range(2, 6):
         rings.append(ring_copy(i, cot_ref.at[i - 1, 0], cot_ref.at[i + 1, 0]))
 
@@ -466,29 +460,35 @@
             rings[first + 2 + way].start()
             core_copy(first + 1 + way).start()
 
+    plan_load.wait()
+
     def step(i):
         blocks = [i * SIDE + j for j in range(SIDE)]
         attend_blocks(
             blocks, list_ref, count_ref, x_ref, kv_ref, kv_t, aq_out, att_t, terms
         )
-        for b in blocks:
-            pl.when(b != seq)(aq_copy(b).start)
         pl.when(i == 0)(lambda: ring_step(0))
 
     each(n_seq // SIDE, step)
     aq_in[seq] = aq_out[seq]
 
-    sums_by_place(plan_ref, 0, terms, running)
-
-    def give(to):
-        halo_grad[to] = sum_of(n_seq + to, plan_ref, 0, running).astype(BF)
-        hg_copy(0, to).start()
-
-    to_grp(give)
+    def sum_up(c):
+        sums_by_place(plan_ref, 0, terms, running, span_of(BACK, c))
+
+    def give(c, to):
+        span = span_of(BACK, c)
+        halo_grad[to, span] = sum_of(n_seq + to, plan_ref, 0, running, span).astype(BF)
+        hg_copy(c, to).start()
+
+    sum_up(0)
+    to_grp(functools.partial(give, 0))
+    to_seq(lambda to: aq_copy(to).start())
+    ring_step(2)
+    for c in range(1, len(BACK)):
+        sum_up(c)
     mine = sum_of(n_seq + grp, plan_ref, 0, running).astype(BF)
     for c in range(len(BACK)):
         back[c][grp] = mine[span_of(BACK, c)]
-    ring_step(2)
 
     def keep(b):
         own_grad[b] = sum_of(b, plan_ref, 0, running)
@@ -512,7 +512,7 @@
         add(slot)
     for c in range(1, len(BACK)):
         all_hg(c - 1).wait_send()
-        to_grp(lambda to, c=c: hg_copy(c, to).start())
+        to_grp(functools.partial(give, c))
     for way in range(2):
         rings[4 + way].wait_recv()
         where = pl.ds(way * middle, middle)
@@ -520,34 +520,37 @@
         rings[-1].start()
         core_copy(5 + way).start()
 
+    stores = []
+
+    def settle(c):
+        span = span_of(BACK, c)
+        all_hg(c).wait_recv()
+        sums_by_place(plan_ref, 4, back[c], back_sum[c])
+
+        def finish(b):
+            more = sum_of(b, plan_ref, 4, back_sum[c])
+            dkv[c][b] = (own_grad[b, span] + more).astype(BF)
+
+        each(n_seq, finish, 4)
+        to_seq(lambda to: dkv_copy(c, to).start())
+        stores.append(local(dkv[c].at[seq], rows_of(kv_back, seq, BACK, c), local_sem.at[2 + c]))
+        stores[-1].start()
+
+    for c in range(len(BACK) - 1):
+        settle(c)
+
     all_aq().wait_recv()
     for j, cols in enumerate(tiles):
         first, second = weave(aq_in[2 * j], aq_in[2 * j + 1])
         q_ref[:, cols] = first.astype(BF)
         att_n[:, cols] = second.astype(BF)
     k_ref[...] = jnp.dot(att_n[...], w_ref[...], preferred_element_type=F32).astype(BF)
-    stores = [local(q_ref, dq_hbm, local_sem.at[0]), local(k_ref, out_hbm, local_sem.at[1])]
-    for store in stores:
+    for store in (local(q_ref, dq_hbm, local_sem.at[0]), local(k_ref, out_hbm, local_sem.at[1])):
         store.start()
+        stores.append(store)
     for slot in range(5, 7):
         add(slot)
 
-    def settle(c):
-        span = span_of(BACK, c)
-        all_hg(c).wait_recv()
-        sums_by_place(plan_ref, 4, back[c], back_sum[c])
-
-        def finish(b):
-            more = sum_of(b, plan_ref, 4, back_sum[c])
-            dkv[c][b] = (own_grad[b, span] + more).astype(BF)
-
-        each(n_seq, finish, 4)
-        to_seq(lambda to: dkv_copy(c, to).start())
-        stores.append(local(dkv[c].at[seq], rows_of(kv_back, seq, BACK, c), local_sem.at[2 + c]))
-        stores[-1].start()
-
-    for c in range(len(BACK) - 1):
-        settle(c)
     for way in range(2):
         rings[6 + way].wait_recv()
     core_copy(7).start()
@@ -589,7 +592,7 @@
         store.wait()
 
 
-def layer(send, lists, counts, plan, q, k, v, cot, weight, n_seq, n_grp):
+def layer(send, lists, counts, q, k, v, cot, weight, n_seq, n_grp):
     rows, width = q.shape
     tile = (rows, LANES)
     per_group = width // n_grp
@@ -599,7 +602,7 @@
     inverse_root = 1.0 / math.sqrt(float(rows * n_seq * n_grp))
     return pl.pallas_call(
         functools.partial(layer_kernel, inverse_root),
-        in_specs=[SMEM] * 4 + [ANY] * 5,
+        in_specs=[SMEM] * 3 + [ANY] * 5,
         out_specs=(ANY, ANY, ANY, VMEM),
         out_shape=(
             shape(q.shape),
@@ -635,7 +638,10 @@
             pltpu.VMEM((n_grp, per_group // 2, LANES), BF),
             pltpu.VMEM((per_group // 2, LANES), F32),
             pltpu.VMEM((n_seq, per_group // 2, LANES), F32),
-            dma((5,)),
+            pltpu.VMEM((items, items), jnp.int32),
+            pltpu.VMEM((8, items), jnp.int32),
+            pltpu.SMEM((8, items), jnp.int32),
+            dma((6,)),
             dma((2 + len(BACK),)),
             dma((8,)),
             dma((8,)),
@@ -661,7 +667,7 @@
         compiler_params=pltpu.CompilerParams(
             vmem_limit_bytes=LIMIT, collective_id=0, has_side_effects=True
         ),
-    )(send, lists, counts, plan, q, k, v, cot, weight)
+    )(send, lists, counts, q, k, v, cot, weight)
 
 
 def finish_kernel(out_in, dq_in, kv_ref, wg_in, out_ref, dq_ref, dk_ref, dv_ref, wg_ref):
@@ -684,7 +690,6 @@
         send,
         lists,
         key_counts,
-        make_plan(send, lists),
         queries,
         key_rows,
         value_rows,

time: 112 us -> 112 us (level); the launches traced: 110 us -> 112 us
  Pallas kernels: 110 us -> 112 us
    pallas_call x1, Pallas kernels: 105 us -> 109 us  [layer(): pl.pallas_call(functools.partial(layer_kernel, inverse_root), in_specs=[S...]
    pallas_call x1 -> x0, Pallas kernels: 2.22 us -> none  [make_plan(): pl.pallas_call(plan_kernel, in_specs=[SMEM] * 2, out_specs=VMEM, out_shap...]
where the time goes in v5:
time: 112 us
  Pallas kernels  112 us (100%)
    pallas_call x1, Pallas kernels, layer(): pl.pallas_call(functools.partial(layer_kernel, inverse_root), in_specs=[S...  109 us
    pallas_call x1, Pallas kernels, per_device(): pl.pallas_call(finish_kernel, in_specs=[VMEM] * 4, out_specs=(VMEM,) * 5,...  2.42 us

profile of v5, /device:TPU:1, one launch (start us, length us, event | category | flops | bytes accessed | tf_op | source)
XLA Modules:
  0.0 112.3 jit_solution(6069312329816402820)
XLA Ops:
  0.6 109.2 %shard_map.119 = (bf16[128,1024]{1,0:T(8,128)(2,1)}, bf16[128,1024]{1,0:T(8,128)(2,1)}, bf16[16,128,128]{2,1,0:T(8,128)(2,1)}, f32[32,1024]{1,0:T(8,128)}) custom-call(s32[1,1,32]{2,1,0:T(1,128)} %bitcast.3, s32[1,8,16]{2,1,0:T(8,128)} %bitcast.2, s32[1,16]{1,0:T(1,128)} %count_ref.1, bf16[128,1024]{1,0:T(8,128)(2,1)} %q_hbm.1, bf16[128,1024]{1,0:T(8,128)(2,1)} %k_hbm.1, ...), custom_call_target="tpu_custom_call" | custom-call | tf_op jit(solution)/shard_map/pallas_call | solution.py:603
  109.9 2.4 %shard_map.120 = (bf16[128,1024]{1,0:T(8,128)(2,1)}, bf16[128,1024]{1,0:T(8,128)(2,1)}, bf16[128,1024]{1,0:T(8,128)(2,1)}, bf16[128,1024]{1,0:T(8,128)(2,1)}, f32[32,1024]{1,0:T(8,128)}) custom-call(bf16[128,1024]{1,0:T(8,128)(2,1)} %get-tuple-element.9.out_in, bf16[128,1024]{1,0:T(8,128)(2,1)} %get-tuple-element.10.dq_in, ...), custom_call_target="tpu_custom_call" | custom-call | tf_op jit(solution)/shard_map/pallas_call | solution.py:702

commit v6 on v5

--- a/solution.py
+++ b/solution.py
@@ -429,8 +429,8 @@
     to_seq(lambda to: qg_copy(to).start())
     pass_on(len(THERE) - 1)
 
-    def turn(i, span=slice(None)):
-        kv_t[i, :, span] = kv_ref[i, span].T
+    def turn(i):
+        kv_t[i] = kv_ref[i].T
 
     each(n_seq, turn, 4)
     make_plan(send_ref, list_ref, place, plan)
@@ -450,7 +450,7 @@
     each(n_seq, prepare, 2)
     for c in range(len(THERE)):
         all_halo(c).wait_recv()
-        each(n_grp, lambda g, c=c: turn(n_seq + g, span_of(THERE, c)), 4)
+    each(n_grp, lambda g: turn(n_seq + g), 4)
     for i in range(2, 6):
         rings.append(ring_copy(i, cot_ref.at[i - 1, 0], cot_ref.at[i + 1, 0]))
 
@@ -467,6 +467,8 @@
         attend_blocks(
             blocks, list_ref, count_ref, x_ref, kv_ref, kv_t, aq_out, att_t, terms
         )
+        for b in blocks:
+            pl.when(b != seq)(aq_copy(b).start)
         pl.when(i == 0)(lambda: ring_step(0))
 
     each(n_seq // SIDE, step)
@@ -482,7 +484,6 @@
 
     sum_up(0)
     to_grp(functools.partial(give, 0))
-    to_seq(lambda to: aq_copy(to).start())
     ring_step(2)
     for c in range(1, len(BACK)):
         sum_up(c)

time: 112 us -> 109 us (0.973)
  Pallas kernels: 112 us -> 109 us
    pallas_call x1, Pallas kernels: 109 us -> 106 us  [layer(): pl.pallas_call(functools.partial(layer_kernel, inverse_root), in_specs=[S...]
where the time goes in v6:
time: 109 us
  Pallas kernels  109 us (100%)
    pallas_call x1, Pallas kernels, layer(): pl.pallas_call(functools.partial(layer_kernel, inverse_root), in_specs=[S...  106 us
    pallas_call x1, Pallas kernels, per_device(): pl.pallas_call(finish_kernel, in_specs=[VMEM] * 4, out_specs=(VMEM,) * 5,...  2.42 us

profile of v6, /device:TPU:1, one launch (start us, length us, event | category | flops | bytes accessed | tf_op | source)
XLA Modules:
  0.0 109.2 jit_solution(12453401756408958918)
XLA Ops:
  0.6 106.1 %shard_map.119 = (bf16[128,1024]{1,0:T(8,128)(2,1)}, bf16[128,1024]{1,0:T(8,128)(2,1)}, bf16[16,128,128]{2,1,0:T(8,128)(2,1)}, f32[32,1024]{1,0:T(8,128)}) custom-call(s32[1,1,32]{2,1,0:T(1,128)} %bitcast.3, s32[1,8,16]{2,1,0:T(8,128)} %bitcast.2, s32[1,16]{1,0:T(1,128)} %count_ref.1, bf16[128,1024]{1,0:T(8,128)(2,1)} %q_hbm.1, bf16[128,1024]{1,0:T(8,128)(2,1)} %k_hbm.1, ...), custom_call_target="tpu_custom_call" | custom-call | tf_op jit(solution)/shard_map/pallas_call | solution.py:604
  106.7 2.4 %shard_map.120 = (bf16[128,1024]{1,0:T(8,128)(2,1)}, bf16[128,1024]{1,0:T(8,128)(2,1)}, bf16[128,1024]{1,0:T(8,128)(2,1)}, bf16[128,1024]{1,0:T(8,128)(2,1)}, f32[32,1024]{1,0:T(8,128)}) custom-call(bf16[128,1024]{1,0:T(8,128)(2,1)} %get-tuple-element.9.out_in, bf16[128,1024]{1,0:T(8,128)(2,1)} %get-tuple-element.10.dq_in, ...), custom_call_target="tpu_custom_call" | custom-call | tf_op jit(solution)/shard_map/pallas_call | solution.py:703
